TPU v7x, 32 devices: a whole 2x2x4 slice. The times are simulated.
32 devices in a mesh: dp: 16 (over z, y, x), tensor: 2 (over core).
Axes of the slice: x: 2, y: 2, z: 4, core: 2. Of those that a mesh axis runs over, the one named last changes fastest.
Arguments:
- arrivals: bfloat16 [16384, 2048], P('dp', 'tensor')
- deal: int32 [16, 32], P('dp'), may hold values from 0 to 511, as said below
- seg_ids: int32 [16, 1024], P('dp'), may hold values from 0 to 7, never falling along the last dimension, each value on 1 to 512 neighbouring positions
- page_table: int32 [16, 8], P('dp'), may hold values from 0 to 7, each once within a row
- attn_gain: float32 [2048], replicated, may hold values from 0.1 to 1.9
- w_query: bfloat16 [2048, 1024], P(None, 'tensor'), may hold values from -0.125 to 0.125
- w_keyval: bfloat16 [2048, 512], replicated, may hold values from -0.125 to 0.125
- query_gain: float32 [64], replicated, may hold values from 0.1 to 1.9
- key_gain: float32 [64], replicated, may hold values from 0.1 to 1.9
- w_out: bfloat16 [1024, 2048], P('tensor'), may hold values from -0.1875 to 0.1875
- ffn_gain: float32 [2048], replicated, may hold values from 0.1 to 1.9
- w_gate: bfloat16 [2048, 5120], P(None, 'tensor'), may hold values from -0.125 to 0.125
- w_up: bfloat16 [2048, 5120], P(None, 'tensor'), may hold values from -0.125 to 0.125
- w_down: bfloat16 [5120, 2048], P('tensor'), may hold values from -0.078125 to 0.078125
Outputs:
- result: bfloat16 [16384, 2048], P('dp', 'tensor')
- kv_pages: bfloat16 [128, 128, 512], P('dp', None, 'tensor')
Inputs may be any that keep to these rules, and one draw needn't show every extreme that they name: deal[s, k] = g * 32 + j sends unit k of arrival block s to unit j of group g; every value occurs once; the units of one arrival block go to exactly 16 groups, 2 units to each. `seg_ids`: each row never falls; one prompt is one run of equal numbers. `page_table`: each row holds every page number once.
All inputs are finite; a program needn't handle non-finite values.
Results may differ from a plain program's by a relative error of at most 0.019.
Values may be sent and summed in bfloat16 or wider, within the bound.
A program may use at most 128 MiB of HBM per device.

v0:
```python
import math

import jax
import jax.numpy as jnp
from jax import lax
from jax.sharding import PartitionSpec as P

HEAD = 64
KVH = 4
MOST = 2
PAGE = 128


EPS = 1e-06
THETA = 10000.0
BLOCK_ROWS = 512


def rms_scale(values, gain):
    values = values.astype(jnp.float32)
    mean_sq = jnp.mean(values * values, axis=-1, keepdims=True)
    return values * lax.rsqrt(mean_sq + EPS) * gain


def rope_tables(positions, width):
    half = width // 2
    inverse = THETA ** (-jnp.arange(half, dtype=jnp.float32) * 2.0 / width)
    angles = positions.astype(jnp.float32)[:, None] * inverse[None, :]
    return (jnp.cos(angles), jnp.sin(angles))


def rotate(values, cosine, sine):
    half = values.shape[-1] // 2
    first = values[..., :half]
    second = values[..., half:]
    cos_b = cosine[:, None, :]
    sin_b = sine[:, None, :]
    return jnp.concatenate(
        [first * cos_b - second * sin_b, second * cos_b + first * sin_b], axis=-1
    )


def segment_starts(seg_row):
    count = seg_row.shape[0]
    index = jnp.arange(count, dtype=jnp.int32)
    prior = jnp.concatenate([seg_row[:1] - 1, seg_row[:-1]])
    marks = jnp.where(seg_row != prior, index, 0)
    return lax.cummax(marks, axis=0)


def on_device(
    arrivals,
    deal,
    seg_ids,
    page_table,
    attn_gain,
    w_query,
    w_keyval,
    query_gain,
    key_gain,
    w_out,
    ffn_gain,
    w_gate,
    w_up,
    w_down,
):
    groups = lax.axis_size("dp")
    shards = lax.axis_size("tensor")
    tensor_rank = lax.axis_index("tensor")
    tok_grp = arrivals.shape[0]
    feat_part = arrivals.shape[1]
    units = deal.shape[1]
    unit_rows = tok_grp // units
    slot_count = groups * MOST
    width = unit_rows * feat_part
    dest_row = deal[0]
    target = dest_row // units
    position = dest_row % units
    unit_index = jnp.arange(units, dtype=jnp.int32)
    earlier = unit_index[:, None] > unit_index[None, :]
    same_target = target[:, None] == target[None, :]
    rank = jnp.sum(jnp.logical_and(earlier, same_target), axis=1)
    slot = target * MOST + rank
    send_hot = slot[None, :] == jnp.arange(slot_count, dtype=jnp.int32)[:, None]
    filled = jnp.any(send_hot, axis=1)
    slot_pos = jnp.where(filled, jnp.sum(jnp.where(send_hot, position[None, :], 0), axis=1), -1)
    send_matrix = send_hot.astype(jnp.bfloat16)
    packed = jnp.dot(
        send_matrix, arrivals.reshape(units, width), preferred_element_type=jnp.float32
    ).astype(jnp.bfloat16)
    received, recv_pos = (
        lax.all_to_all(
            packed.reshape(groups, MOST, width), "dp", split_axis=0, concat_axis=0, tiled=True
        ),
        lax.all_to_all(
            slot_pos.reshape(groups, MOST), "dp", split_axis=0, concat_axis=0, tiled=True
        ),
    )
    recv_matrix = (recv_pos.reshape(-1)[None, :] == unit_index[:, None]).astype(jnp.bfloat16)
    grouped = jnp.dot(
        recv_matrix, received.reshape(slot_count, width), preferred_element_type=jnp.float32
    ).astype(jnp.bfloat16)
    grouped = grouped.reshape(tok_grp, feat_part)
    full = lax.all_gather(grouped, "tensor", axis=1, tiled=True)
    normed = rms_scale(full, attn_gain).astype(jnp.bfloat16)
    seg_row = seg_ids[0]
    starts = segment_starts(seg_row)
    index = jnp.arange(tok_grp, dtype=jnp.int32)
    cosine, sine = rope_tables(index - starts, HEAD)
    q_heads = w_query.shape[1] // HEAD
    q_raw = jnp.dot(normed, w_query, preferred_element_type=jnp.float32).reshape(
        tok_grp, q_heads, HEAD
    )
    queries = rotate(rms_scale(q_raw, query_gain), cosine, sine).astype(jnp.bfloat16)
    kv_heads = max(1, KVH // shards)
    kv_first = tensor_rank * KVH // shards
    kv_weight = lax.dynamic_slice_in_dim(w_keyval, kv_first * 2 * HEAD, kv_heads * 2 * HEAD, 1)
    kv_raw = jnp.dot(normed, kv_weight, preferred_element_type=jnp.float32).reshape(
        tok_grp, kv_heads, 2, HEAD
    )
    keys = rotate(rms_scale(kv_raw[:, :, 0], key_gain), cosine, sine).astype(jnp.bfloat16)
    values = kv_raw[:, :, 1].astype(jnp.bfloat16)
    stacked = jnp.stack([keys, values], axis=2).reshape(tok_grp, kv_heads * 2 * HEAD)
    cache_cols = 2 * KVH * HEAD // shards
    offset = tensor_rank * cache_cols - kv_first * 2 * HEAD
    own_cache = lax.dynamic_slice_in_dim(stacked, offset, cache_cols, 1)
    pages = own_cache.reshape(tok_grp // PAGE, PAGE, cache_cols)
    kv_pages = jnp.zeros_like(pages).at[page_table[0]].set(pages)
    share = q_heads // kv_heads
    grouped_q = queries.reshape(tok_grp, kv_heads, share, HEAD)
    scale = 1.0 / math.sqrt(HEAD)
    block = min(BLOCK_ROWS, tok_grp)
    outputs = []
    for first in range(0, tok_grp, block):
        last = first + block
        scores = (
            jnp.einsum(
                "ikgd,jkd->kgij",
                grouped_q[first:last],
                keys[:last],
                preferred_element_type=jnp.float32,
            )
            * scale
        )
        query_rows = index[first:last]
        allowed = jnp.logical_and(
            query_rows[:, None] >= index[None, :last],
            starts[first:last][:, None] <= index[None, :last],
        )
        weights = jnp.where(allowed, jnp.exp(scores), 0.0)
        probs = (weights / jnp.sum(weights, axis=-1, keepdims=True)).astype(jnp.bfloat16)
        mixed = jnp.einsum(
            "kgij,jkd->ikgd", probs, values[:last], preferred_element_type=jnp.float32
        )
        outputs.append(mixed.astype(jnp.bfloat16).reshape(block, q_heads * HEAD))
    attended = jnp.concatenate(outputs, axis=0)
    attn_sum = lax.psum(
        jnp.dot(attended, w_out, preferred_element_type=jnp.float32).astype(jnp.bfloat16), "tensor"
    ).astype(jnp.float32)
    middle = (full.astype(jnp.float32) + attn_sum).astype(jnp.bfloat16)
    ffn_in = rms_scale(middle, ffn_gain).astype(jnp.bfloat16)
    gate = jnp.dot(ffn_in, w_gate, preferred_element_type=jnp.float32)
    upper = jnp.dot(ffn_in, w_up, preferred_element_type=jnp.float32)
    hidden = (jax.nn.silu(gate) * upper).astype(jnp.bfloat16)
    ffn_part = lax.psum_scatter(
        jnp.dot(hidden, w_down, preferred_element_type=jnp.float32).astype(jnp.bfloat16),
        "tensor",
        scatter_dimension=1,
        tiled=True,
    ).astype(jnp.float32)
    own_cols = lax.dynamic_slice_in_dim(middle, tensor_rank * feat_part, feat_part, 1)
    combined = (own_cols.astype(jnp.float32) + ffn_part).astype(jnp.bfloat16)
    back = jnp.dot(
        recv_matrix.T, combined.reshape(units, width), preferred_element_type=jnp.float32
    ).astype(jnp.bfloat16)
    returned = lax.all_to_all(
        back.reshape(groups, MOST, width), "dp", split_axis=0, concat_axis=0, tiled=True
    )
    result = jnp.dot(
        send_matrix.T, returned.reshape(slot_count, width), preferred_element_type=jnp.float32
    ).astype(jnp.bfloat16)
    return (result.reshape(tok_grp, feat_part), kv_pages)


def solution(mesh):
    return jax.shard_map(
        on_device,
        mesh=mesh,
        in_specs=(
            P("dp", "tensor"),
            P("dp", None),
            P("dp", None),
            P("dp", None),
            P(),
            P(None, "tensor"),
            P(),
            P(),
            P(),
            P("tensor", None),
            P(),
            P(None, "tensor"),
            P(None, "tensor"),
            P("tensor", None),
        ),
        out_specs=(P("dp", "tensor"), P("dp", None, "tensor")),
        check_vma=False,
    )
```

profile of v0, /device:TPU:12, one launch (start us, length us, event | category | flops | bytes accessed | tf_op | source)
XLA Modules:
  0.0 321.9 jit_solution(5833053653207537025)
XLA Ops:
  7.2 0.8 fusion.47
  8.0 0.7 and_select_fusion.1
  9.1 0.7 select_n.79
  9.8 7.2 %all-to-all-start = ((s32[16,1,2]{2,1,0:T(1,128)}), s32[16,1,2]{2,1,0:T(1,128)S(1)}, u32[]{:S(2)}, u32[]{:S(2)}) async-start(s32[16,1,2]{2,1,0:T(1,128)} %bitcast.5), calls=%async_computation | async-start | bytes 16384 | tf_op jit(solution)/shard_map/all_to_all | solution.py:95
  17.0 4.2 %reshape.298 = bf16[32,32768]{1,0:T(8,128)(2,1)} reshape(bf16[1024,1024]{1,0:T(8,128)(2,1)} %param.14) | data formatting | bytes 4194304 | tf_op jit(solution)/shard_map/reshape | solution.py:89
  21.1 3.6 %convolution_convert_fusion.3 = bf16[32,32768]{1,0:T(8,128)(2,1)} fusion(bf16[32,32768]{1,0:T(8,128)(2,1)} %reshape.298, s32[32]{0:T(128)S(1)} %fusion.49), kind=kOutput, calls=%fused_computation.4 | convolution fusion | flops 68158464 | bytes 4194432 | tf_op jit(solution)/shard_map/dot_general | solution.py:88
  24.8 4.4 %reshape.299 = bf16[16,2,32768]{2,1,0:T(2,128)(2,1)} reshape(bf16[32,32768]{1,0:T(8,128)(2,1)} %convolution_convert_fusion.3) | data formatting | bytes 4194304 | tf_op jit(solution)/shard_map/reshape | solution.py:93
  29.2 6.9 %all-to-all-start.1 = ((bf16[16,2,32768]{2,1,0:T(2,128)(2,1)}), bf16[16,2,32768]{2,1,0:T(2,128)(2,1)}, u32[]{:S(2)}, u32[]{:S(2)}) async-start(bf16[16,2,32768]{2,1,0:T(2,128)(2,1)} %reshape.299), calls=%async_computation.1 | async-start | bytes 4194304 | tf_op jit(solution)/shard_map/all_to_all | solution.py:92
  36.1 0.5 broadcast.232
  36.6 0.7 reduce.5
  37.4 46.6 %all-to-all-done.1 = bf16[16,2,32768]{2,1,0:T(2,128)(2,1)} async-done(((bf16[16,2,32768]{2,1,0:T(2,128)(2,1)}), bf16[16,2,32768]{2,1,0:T(2,128)(2,1)}, u32[]{:S(2)}, u32[]{:S(2)}) %all-to-all-start.1) | async-done | bytes 2097184 | tf_op jit(solution)/shard_map/all_to_all | solution.py:92
  84.0 4.1 %reshape.300 = bf16[32,32768]{1,0:T(8,128)(2,1)} reshape(bf16[16,2,32768]{2,1,0:T(2,128)(2,1)} %all-to-all-done.1) | data formatting | bytes 4194304 | tf_op jit(solution)/shard_map/reshape | solution.py:101
  88.1 3.6 %convolution_convert_fusion.2 = bf16[32,32768]{1,0:T(8,128)(2,1)} fusion(bf16[32,32768]{1,0:T(8,128)(2,1)} %reshape.300, s32[32]{0:T(128)S(1)} %eq.50), kind=kOutput, calls=%fused_computation.3 | convolution fusion | flops 68158464 | bytes 4194432 | tf_op jit(solution)/shard_map/dot_general | solution.py:100
  91.8 4.2 %reshape.301 = bf16[1024,1024]{1,0:T(8,128)(2,1)} reshape(bf16[32,32768]{1,0:T(8,128)(2,1)} %convolution_convert_fusion.2) | data formatting | bytes 4194304 | tf_op jit(solution)/shard_map/reshape | solution.py:103
  96.0 0.6 all-reduce.2.cloned.1.call-start
  96.6 0.5 slice.78
  98.5 0.5 multiply_cosine_fusion
  99.0 1.0 compare_and_fusion
  100.0 0.5 fusion.14
  100.5 8.2 %all-gather.2.cloned.1.call-done = bf16[1024,2048]{1,0:T(8,128)(2,1)} async-done(((bf16[1024,1024]{1,0:T(8,128)(2,1)}), bf16[1024,2048]{1,0:T(8,128)(2,1)}) %all-gather.2.cloned.1.call-update) | async-done | bytes 4194320 | tf_op jit(solution)/shard_map/all_gather | solution.py:104
  108.7 3.2 %fusion.4 = f32[1024]{0:T(1024)S(1)} fusion(bf16[1024,2048]{1,0:T(8,128)(2,1)} %all-gather.2.cloned.1.call-done), kind=kLoop, calls=%fused_computation.17 | loop fusion | flops 6290432 | bytes 4198400 | tf_op jit(solution)/shard_map/reduce_sum | solution.py:21
  112.2 3.0 fusion.23
  115.3 2.6 multiply_reduce_fusion
  118.2 0.4 multiply_multiply_fusion
  118.6 0.3 subtract_convert_fusion
  119.1 4.2 %fusion = (f32[2,4,512]{2,1,0:T(4,128)S(1)}, f32[2,1024,512,4]{2,1,3,0:T(8,128)S(1)}) fusion(pred[512,1024]{0,1:T(8,128)(4,1)S(1)} %fusion.14, bf16[512,2,4,64]{0,3,2,1:T(8,128)(2,1)S(1)} %bitcast.129, bf16[1024,2,32]{0,2,1:T(8,128)(2,1)S(1)} %get-tuple-element.11, bf16[1024,2,32]{0,2,1:T(8,128)(2,1)S(1)} %get-tuple-element.10), kind=kOutput, calls=%fused_computation.7 | convolution fusion | flops 549974016 | bytes 18104320 | tf_op jit(solution)/shard_map/ikgd,jkd->kgij/dot_general | solution.py:137
  123.4 4.3 %fusion.16 = bf16[2,64,4,512]{3,1,2,0:T(8,128)(2,1)S(1)} fusion(f32[2,1024,512,4]{2,1,3,0:T(8,128)S(1)} %get-tuple-element.21, f32[2,4,512]{2,1,0:T(4,128)S(1)} %get-tuple-element.20, pred[512,1024]{0,1:T(8,128)(4,1)S(1)} %fusion.14, f32[1024,2,2,64]{0,3,2,1:T(8,128)S(1)} %bitcast.127), kind=kOutput, calls=%fused_computation.37 | convolution fusion | flops 553910272 | bytes 18104320 | tf_op jit(solution)/shard_map/kgij,jkd->ikgd/dot_general | solution.py:152
  127.7 2.2 fusion.10
  129.9 2.2 fusion.15
  132.1 4.4 %convolution_convert_fusion.4 = bf16[1024,2048]{1,0:T(8,128)(2,1)} fusion(bf16[512,2048]{1,0:T(8,128)(2,1)S(1)} %copy-done, bf16[512,512]{0,1:T(8,128)(2,1)S(1)} %bitcast.134, bf16[512,512]{0,1:T(8,128)(2,1)S(1)} %bitcast.135), kind=kOutput, calls=%fused_computation.29 | convolution fusion | flops 2151677952 | bytes 7340032 | tf_op jit(solution)/shard_map/dot_general | solution.py:158
  136.5 29.7 %all-reduce.2.cloned.1.call-done = bf16[1024,2048]{1,0:T(8,128)(2,1)} async-done(((bf16[1024,2048]{1,0:T(8,128)(2,1)}), bf16[1024,2048]{1,0:T(8,128)(2,1)}) %all-reduce.2.cloned.1.call-update) | async-done | bytes 4194320 | tf_op jit(solution)/shard_map/psum | solution.py:157
  166.2 5.5 %fusion.1 = (f32[1024]{0:T(1024)S(1)}, bf16[1024,2048]{1,0:T(8,128)(2,1)S(1)}) fusion(bf16[1024,2048]{1,0:T(8,128)(2,1)} %all-reduce.2.cloned.1.call-done, bf16[1024,2048]{1,0:T(8,128)(2,1)} %all-gather.2.cloned.1.call-done), kind=kLoop, calls=%fused_computation.14 | loop fusion | flops 14679040 | bytes 12587008 | tf_op jit(solution)/shard_map/reduce_sum | solution.py:21
  171.7 2.1 copy-done.3
  173.8 16.4 %fusion.19 = f32[1024,2560]{1,0:T(8,128)} fusion(bf16[2048,2560]{1,0:T(8,128)(2,1)} %param.25, bf16[1024,2048]{1,0:T(8,128)(2,1)S(1)} %get-tuple-element.3, f32[2048]{0:T(1024)S(1)} %copy-done.13, f32[1024]{0:T(1024)S(1)} %add_rsqrt_fusion.2), kind=kOutput, calls=%fused_computation.38 | convolution fusion | flops 10745806848 | bytes 25178112 | tf_op jit(solution)/shard_map/dot_general | solution.py:162
  190.2 33.0 %fusion.13 = bf16[1024,2048]{1,0:T(8,128)(2,1)} fusion(bf16[2560,2048]{1,0:T(8,128)(2,1)} %param.27, f32[1024,2560]{1,0:T(8,128)} %fusion.19, bf16[2048,2560]{1,0:T(8,128)(2,1)} %param.26, bf16[1024,2048]{1,0:T(8,128)(2,1)} %copy-done.3, f32[2048]{0:T(1024)S(1)} %copy-done.13, f32[1024]{0:T(1024)S(1)} %add_rsqrt_fusion.2), kind=kOutput, calls=%fused_computation.30 | convolution fusion | flops 21501050880 | bytes 39858176 | tf_op jit(solution)/shard_map/dot_general | solution.py:166
  223.2 13.5 %reduce-scatter.2.cloned.1.call-done = bf16[1024,1024]{1,0:T(8,128)(2,1)} async-done(((bf16[1024,2048]{1,0:T(8,128)(2,1)}), bf16[1024,1024]{1,0:T(8,128)(2,1)}) %reduce-scatter.2.cloned.1.call-update) | async-done | bytes 2097168 | tf_op jit(solution)/shard_map/reduce_scatter | solution.py:165
  236.7 3.2 add_convert_fusion
  239.9 2.6 reshape.307
  242.4 2.3 convolution_convert_fusion.1
  244.8 2.6 reshape.308
  247.4 7.0 %all-to-all-start.2 = ((bf16[16,2,32768]{2,1,0:T(2,128)(2,1)}), bf16[16,2,32768]{2,1,0:T(2,128)(2,1)}, u32[]{:S(2)}, u32[]{:S(2)}) async-start(bf16[16,2,32768]{2,1,0:T(2,128)(2,1)} %reshape.308), calls=%async_computation.3 | async-start | bytes 4194304 | tf_op jit(solution)/shard_map/all_to_all | solution.py:176
  254.5 0.8 copy.46
  255.3 0.7 reshape.324
  256.0 0.8 scatter_fusion
  256.8 46.1 %all-to-all-done.2 = bf16[16,2,32768]{2,1,0:T(2,128)(2,1)} async-done(((bf16[16,2,32768]{2,1,0:T(2,128)(2,1)}), bf16[16,2,32768]{2,1,0:T(2,128)(2,1)}, u32[]{:S(2)}, u32[]{:S(2)}) %all-to-all-start.2) | async-done | bytes 2097184 | tf_op jit(solution)/shard_map/all_to_all | solution.py:176
  302.9 4.3 %reshape.309 = bf16[32,32768]{1,0:T(8,128)(2,1)} reshape(bf16[16,2,32768]{2,1,0:T(2,128)(2,1)} %all-to-all-done.2) | data formatting | bytes 4194304 | tf_op jit(solution)/shard_map/reshape | solution.py:180
  307.2 3.7 %convolution_convert_fusion = bf16[32,32768]{1,0:T(8,128)(2,1)} fusion(bf16[32,32768]{1,0:T(8,128)(2,1)} %reshape.309, s32[32]{0:T(128)S(1)} %copy-done.8), kind=kOutput, calls=%fused_computation.1 | convolution fusion | flops 68158464 | bytes 4194432 | tf_op jit(solution)/shard_map/dot_general | solution.py:179
  310.9 4.2 %reshape.310 = bf16[1024,1024]{1,0:T(8,128)(2,1)} reshape(bf16[32,32768]{1,0:T(8,128)(2,1)} %convolution_convert_fusion) | data formatting | bytes 4194304 | tf_op jit(solution)/shard_map/reshape | solution.py:182
  (65 shorter events, 2.1 us)
Async XLA Ops:
  7.2 124.9 %copy-start = (bf16[512,2048]{1,0:T(8,128)(2,1)S(1)}, bf16[512,2048]{1,0:T(8,128)(2,1)}, u32[]{:S(2)}) copy-start(bf16[512,2048]{1,0:T(8,128)(2,1)} %param.23) | copy-start | bytes 6291460
  8.8 15.9 %copy-start.7 = (s32[32]{0:T(128)}, s32[32]{0:T(128)S(1)}, u32[]{:S(2)}) copy-start(s32[32]{0:T(128)S(1)} %fusion.49) | copy-start | bytes 388
  9.8 19.4 %all-to-all-start = ((s32[16,1,2]{2,1,0:T(1,128)}), s32[16,1,2]{2,1,0:T(1,128)S(1)}, u32[]{:S(2)}, u32[]{:S(2)}) async-start(s32[16,1,2]{2,1,0:T(1,128)} %bitcast.5), calls=%async_computation | async-start | bytes 16384 | tf_op jit(solution)/shard_map/all_to_all | solution.py:95
  29.2 54.9 %all-to-all-start.1 = ((bf16[16,2,32768]{2,1,0:T(2,128)(2,1)}), bf16[16,2,32768]{2,1,0:T(2,128)(2,1)}, u32[]{:S(2)}, u32[]{:S(2)}) async-start(bf16[16,2,32768]{2,1,0:T(2,128)(2,1)} %reshape.299), calls=%async_computation.1 | async-start | bytes 4194304 | tf_op jit(solution)/shard_map/all_to_all | solution.py:92
  36.1 72.6 %all-gather.2.cloned.1.call-start = ((), (), s32[]{:S(2)}) async-start(), calls=%async_computation.4 | async-start | bytes 6291456 | tf_op jit(solution)/shard_map/all_gather | solution.py:104
  91.8 4.8 %copy-start.6 = (s32[1,1024]{1,0:T(1,128)S(1)}, s32[1,1024]{1,0:T(1,128)}, u32[]{:S(2)}) copy-start(s32[1,1024]{1,0:T(1,128)} %param.16) | copy-start | bytes 12292
  96.0 16.0 %copy-start.12 = (f32[2048]{0:T(1024)S(1)}, f32[2048]{0:T(1024)}, u32[]{:S(2)}) copy-start(f32[2048]{0:T(1024)} %param.18) | copy-start | bytes 24580
  96.0 70.2 %all-reduce.2.cloned.1.call-start = ((), (), s32[]{:S(2)}) async-start(), calls=%async_computation.5 | async-start | bytes 8388608 | tf_op jit(solution)/shard_map/psum | solution.py:157
  108.7 3.4 %copy-start.2 = (bf16[1024,2048]{1,0:T(8,128)(2,1)S(1)}, bf16[1024,2048]{1,0:T(8,128)(2,1)}, u32[]{:S(2)}) copy-start(bf16[1024,2048]{1,0:T(8,128)(2,1)} %all-gather.2.cloned.1.call-done) | copy-start | bytes 12582916
  112.2 3.1 copy-start.11
  115.3 2.7 copy-start.9
  115.3 2.8 copy-start.10
  123.3 4.3 %copy-start.5 = (pred[512,512]{0,1:T(8,128)(4,1)S(1)}, pred[512,512]{0,1:T(8,128)(4,1)}, u32[]{:S(2)}) copy-start(pred[512,512]{0,1:T(8,128)(4,1)} %compare_and_fusion) | copy-start | bytes 786436
  136.5 37.3 %copy-start.13 = (f32[2048]{0:T(1024)S(1)}, f32[2048]{0:T(1024)}, u32[]{:S(2)}) copy-start(f32[2048]{0:T(1024)} %param.24) | copy-start | bytes 24580
  136.5 100.2 %reduce-scatter.2.cloned.1.call-start = ((), (), s32[]{:S(2)}) async-start(), calls=%async_computation.6 | async-start | bytes 6291456 | tf_op jit(solution)/shard_map/reduce_scatter | solution.py:165
  171.7 2.1 copy-start.3
  244.8 9.6 %copy-start.14 = (s32[1,8]{1,0:T(1,128)S(1)}, s32[1,8]{1,0:T(1,128)}, u32[]{:S(2)}) copy-start(s32[1,8]{1,0:T(1,128)} %param.17) | copy-start | bytes 100
  247.4 55.5 %all-to-all-start.2 = ((bf16[16,2,32768]{2,1,0:T(2,128)(2,1)}), bf16[16,2,32768]{2,1,0:T(2,128)(2,1)}, u32[]{:S(2)}, u32[]{:S(2)}) async-start(bf16[16,2,32768]{2,1,0:T(2,128)(2,1)} %reshape.308), calls=%async_computation.3 | async-start | bytes 4194304 | tf_op jit(solution)/shard_map/all_to_all | solution.py:176
  255.3 51.9 %copy-start.8 = (s32[32]{0:T(128)S(1)}, s32[32]{0:T(128)}, u32[]{:S(2)}) copy-start(s32[32]{0:T(128)} %copy-done.7) | copy-start | bytes 388
  256.8 54.1 %copy-start.4 = (bf16[8,128,256]{2,1,0:T(8,128)(2,1)}, bf16[8,128,256]{2,1,0:T(8,128)(2,1)S(1)}, u32[]{:S(2)}) copy-start(bf16[8,128,256]{2,1,0:T(8,128)(2,1)S(1)} %scatter_fusion) | copy-start | bytes 1572868
  302.9 12.2 %copy-start.1 = (bf16[512,2048]{1,0:T(8,128)(2,1)S(1)}, bf16[512,2048]{1,0:T(8,128)(2,1)}, u32[]{:S(2)}) copy-start(bf16[512,2048]{1,0:T(8,128)(2,1)} %param.23) | copy-start | bytes 6291460
Sparse Core Ops, SparseCore 0:
  96.1 12.5 all-gather.1
  136.6 29.5 all-reduce.1
  223.3 13.3 reduce-scatter.1
where the time goes:
time: 326 us; the launch traced here: 322 us
  waiting for transfers between devices  144 us (44%)
  matrix products  85.6 us (26%)
  local copies, waits for them, and re-layouts  37.2 us (11%)
  starting transfers between devices  21.7 us (7%)
  other arithmetic  18.1 us (6%)
  between operations  15.1 us (5%)
    all_to_all x1, waiting for transfers between devices, on_device(): lax.all_to_all(packed.reshape(groups, MOST, width), 'dp', split_axis=0, c...  46.6 us
    all_to_all x1, waiting for transfers between devices, on_device(): lax.all_to_all(back.reshape(groups, MOST, width), 'dp', split_axis=0, con...  46.1 us
    dot_general x1, matrix products, on_device(): jnp.dot(hidden, w_down, preferred_element_type=jnp.float32)  33 us
    psum x1, waiting for transfers between devices, on_device(): lax.psum(jnp.dot(attended, w_out, preferred_element_type=jnp.float32).ast...  29.7 us
    dot_general x1, matrix products, on_device(): gate = jnp.dot(ffn_in, w_gate, preferred_element_type=jnp.float32)  16.4 us
    reduce_scatter x1, waiting for transfers between devices, on_device(): lax.psum_scatter(jnp.dot(hidden, w_down, preferred_element_type=jnp.float...  13.5 us
    reduce_sum x3, other arithmetic, rms_scale(): mean_sq = jnp.mean(values * values, axis=-1, keepdims=True)  8.75 us
    all_gather x1, waiting for transfers between devices, on_device(): full = lax.all_gather(grouped, 'tensor', axis=1, tiled=True)  8.17 us
  transfers between devices with their start and end apart: 6, of which 5 were waited for; matrix products, arithmetic and copies ran while one was open for 6% of the time, Pallas kernels for 0%

commit v1 on v0

v1 whole, which is shorter than its diff:
```python
import functools
import math

import jax
import jax.numpy as jnp
from jax import lax
from jax.experimental import pallas as pl
from jax.experimental.pallas import tpu as pltpu
from jax.sharding import PartitionSpec as P

HEAD = 64
KVH = 4
MOST = 2
PAGE = 128
WINDOW = 512
EPS = 1e-06
THETA = 10000.0
LANES = 128
TILE = 256
VMEM_LIMIT = 60 * 1024 * 1024

VMEM = pl.BlockSpec(memory_space=pltpu.VMEM)
SMEM = pl.BlockSpec(memory_space=pltpu.SMEM)


def segment_starts(seg_row):
    count = seg_row.shape[0]
    index = jnp.arange(count, dtype=jnp.int32)
    prior = jnp.concatenate([seg_row[:1] - 1, seg_row[:-1]])
    marks = jnp.where(seg_row != prior, index, 0)
    return lax.cummax(marks, axis=0)


def qkv_kernel(unit_rows, slots, src, x, gain, wq, wkv, hgain, normed_cols, mean_mat, out, held):
    step = pl.program_id(0)
    rows = x.shape[0]
    qcols = wq.shape[1]
    cols = qcols + wkv.shape[1]
    xv = x[...].astype(jnp.float32)
    ms = jnp.mean(xv * xv, axis=-1, keepdims=True)
    xn = (xv * lax.rsqrt(ms + EPS) * gain[...]).astype(jnp.bfloat16)
    q = jnp.dot(xn, wq[...], preferred_element_type=jnp.float32)
    kv = jnp.dot(xn, wkv[...], preferred_element_type=jnp.float32)
    here = pl.ds(pl.multiple_of(step * rows, rows), rows)
    for first in range(0, cols, LANES):
        if first < qcols:
            part = q[:, first : first + LANES]
        else:
            part = kv[:, first - qcols : first - qcols + LANES]
        mean = jnp.dot(
            (part * part).astype(jnp.bfloat16), mean_mat[...], preferred_element_type=jnp.float32
        )
        at = slice(first, first + LANES)
        scaled = part * lax.rsqrt(mean + EPS) * hgain[:, at]
        held[here, at] = jnp.where(normed_cols[:, at] > 0.5, scaled, part).astype(jnp.bfloat16)

    @pl.when(step == pl.num_programs(0) - 1)
    def _():
        def move(slot, carry):
            frm = pl.multiple_of(src[slot] * unit_rows, unit_rows)
            to = pl.multiple_of(slot * unit_rows, unit_rows)
            out[pl.ds(to, unit_rows), :] = held[pl.ds(frm, unit_rows), :]
            return carry

        lax.fori_loop(0, slots, move, 0)


def attention_kernel(
    unit_rows, slots, qcols, slot_of, pos_of, table, recv, cosq, sinq, coskv, sinkv, starts, rot,
    pages, back, got, qs, kvs, att
):
    tokens, cols = got.shape
    units = tokens // unit_rows

    def fetch(unit, carry):
        frm = pl.multiple_of(slot_of[unit] * unit_rows, unit_rows)
        to = pl.multiple_of(unit * unit_rows, unit_rows)
        got[pl.ds(to, unit_rows), :] = recv[pl.ds(frm, unit_rows), :]
        return carry

    lax.fori_loop(0, units, fetch, 0)
    scale = math.log2(math.e) / math.sqrt(HEAD)
    for first in range(0, cols, LANES):
        at = slice(first, first + LANES)
        part = got[:, at]
        turned = jnp.dot(part, rot[...], preferred_element_type=jnp.float32)
        part = part.astype(jnp.float32)
        if first < qcols:
            qs[:, at] = ((part * cosq[...] + turned * sinq[...]) * scale).astype(jnp.bfloat16)
        else:
            kvs[:, first - qcols : first - qcols + LANES] = (
                part * coskv[...] + turned * sinkv[...]
            ).astype(jnp.bfloat16)
    page_rows = pages.shape[1]

    def page(p, carry):
        pages[table[p], :, :] = kvs[pl.ds(pl.multiple_of(p * page_rows, page_rows), page_rows), :]
        return carry

    lax.fori_loop(0, pages.shape[0], page, 0)

    kv_heads = kvs.shape[1] // LANES
    pairs = qcols // LANES // kv_heads
    low = lax.broadcasted_iota(jnp.int32, (1, LANES), 1) < HEAD
    for head in range(kv_heads):
        kv = kvs[:, head * LANES : (head + 1) * LANES].astype(jnp.float32)
        kvr = pltpu.roll(kv, HEAD, 1)
        key_e = kv.astype(jnp.bfloat16)
        key_o = kvr.astype(jnp.bfloat16)
        val_e = jnp.where(low, kvr, 1.0).astype(jnp.bfloat16)
        val_o = jnp.where(low, 1.0, kv).astype(jnp.bfloat16)
        for i0 in range(0, tokens, TILE):
            j0 = max(0, i0 - WINDOW)
            i1 = i0 + TILE
            rows = lax.broadcasted_iota(jnp.int32, (TILE, i1 - j0), 0) + i0
            keys = lax.broadcasted_iota(jnp.int32, (TILE, i1 - j0), 1) + j0
            allowed = jnp.logical_and(rows >= keys, starts[i0:i1, :] <= keys)
            bias = jnp.where(allowed, 0.0, -1e30)
            for pair in range(pairs):
                at = slice((head * pairs + pair) * LANES, (head * pairs + pair + 1) * LANES)
                q = qs[i0:i1, at]
                outs = []
                for keep, key, val in ((low, key_e, val_e), (jnp.logical_not(low), key_o, val_o)):
                    qm = jnp.where(keep, q, jnp.zeros_like(q))
                    s = lax.dot_general(
                        qm, key[j0:i1], (((1,), (1,)), ((), ())), preferred_element_type=jnp.float32
                    )
                    w = jnp.exp2(s + bias).astype(jnp.bfloat16)
                    outs.append(jnp.dot(w, val[j0:i1], preferred_element_type=jnp.float32))
                even, odd = outs
                den = pltpu.roll(jnp.where(low, odd, even), HEAD, 1)
                att[i0:i1, at] = (jnp.where(low, even, odd) / den).astype(jnp.bfloat16)

    def give(slot, carry):
        frm = pl.multiple_of(pos_of[slot] * unit_rows, unit_rows)
        to = pl.multiple_of(slot * unit_rows, unit_rows)
        back[pl.ds(to, unit_rows), :] = att[pl.ds(frm, unit_rows), :]
        return carry

    lax.fori_loop(0, slots, give, 0)


def gather_kernel(unit_rows, slot_of, came, out):
    def fetch(unit, carry):
        frm = pl.multiple_of(slot_of[unit] * unit_rows, unit_rows)
        to = pl.multiple_of(unit * unit_rows, unit_rows)
        out[pl.ds(to, unit_rows), :] = came[pl.ds(frm, unit_rows), :]
        return carry

    lax.fori_loop(0, out.shape[0] // unit_rows, fetch, 0)


def ffn_kernel(
    nf, rank, x, att, wo, gain, wg, wu, wd, part, mid, ffn_in, hidden
):
    step = pl.program_id(0)
    tokens = x.shape[0]
    fp = mid.shape[1]
    ft = wg.shape[1]

    @pl.when(step == 0)
    def _():
        own = pl.ds(pl.multiple_of(rank[0] * fp, fp), fp)

        def rows(i, carry):
            at = pl.ds(pl.multiple_of(i * TILE, TILE), TILE)
            total = jnp.dot(att[at, :], wo[...], preferred_element_type=jnp.float32)
            middle = (x[at, :].astype(jnp.float32) + total).astype(jnp.bfloat16)
            ffn_in[at, :] = middle
            mid[at, :] = ffn_in[at, own]
            m = middle.astype(jnp.float32)
            ms = jnp.mean(m * m, axis=-1, keepdims=True)
            ffn_in[at, :] = (m * lax.rsqrt(ms + EPS) * gain[...]).astype(jnp.bfloat16)
            return carry

        lax.fori_loop(0, tokens // TILE, rows, 0)

    @pl.when(step < nf)
    def _():
        cols = pl.ds(pl.multiple_of(step * ft, ft), ft)

        def rows(i, carry):
            at = pl.ds(pl.multiple_of(i * TILE, TILE), TILE)
            g = jnp.dot(ffn_in[at, :], wg[...], preferred_element_type=jnp.float32)
            u = jnp.dot(ffn_in[at, :], wu[...], preferred_element_type=jnp.float32)
            hidden[at, cols] = (g / (1.0 + jnp.exp(-g)) * u).astype(jnp.bfloat16)
            return carry

        lax.fori_loop(0, tokens // TILE, rows, 0)

    @pl.when(step >= nf)
    def _():
        def rows(i, carry):
            at = pl.ds(pl.multiple_of(i * TILE, TILE), TILE)
            part[at, :] = jnp.dot(
                hidden[at, :], wd[...], preferred_element_type=jnp.float32
            ).astype(jnp.bfloat16)
            return carry

        lax.fori_loop(0, tokens // TILE, rows, 0)


def on_device(
    arrivals, deal, seg_ids, page_table, attn_gain, w_query, w_keyval, query_gain, key_gain,
    w_out, ffn_gain, w_gate, w_up, w_down,
):
    groups = lax.axis_size("dp")
    shards = lax.axis_size("tensor")
    me = lax.axis_index("dp")
    rank_t = lax.axis_index("tensor")
    tokens, fp = arrivals.shape
    units = deal.shape[1]
    unit_rows = tokens // units
    slots = groups * MOST
    width = fp * shards
    qcols = w_query.shape[1]
    kv_heads = max(1, KVH // shards)
    kv_first = rank_t * KVH // shards
    cache_cols = 2 * KVH * HEAD // shards
    kvcols = 2 * HEAD * kv_heads
    cols = qcols + kvcols
    params = pltpu.CompilerParams(vmem_limit_bytes=VMEM_LIMIT)

    full = lax.all_gather(arrivals, "tensor", axis=1, tiled=True)
    deal_all = lax.all_gather(deal[0], "dp", axis=0)
    wo_full = lax.all_gather(w_out, "tensor", axis=0, tiled=True)

    dest_row = deal[0]
    target = dest_row // units
    unit_index = jnp.arange(units, dtype=jnp.int32)
    earlier = unit_index[:, None] > unit_index[None, :]
    rank = jnp.sum(jnp.logical_and(earlier, target[:, None] == target[None, :]), axis=1)
    slot = (target * MOST + rank).astype(jnp.int32)
    slot_index = jnp.arange(slots, dtype=jnp.int32)
    hot = slot[None, :] == slot_index[:, None]
    src = jnp.sum(jnp.where(hot, unit_index[None, :], 0), axis=1).astype(jnp.int32)

    mine = deal_all // units == me
    place = deal_all % units
    before = jnp.sum(
        jnp.logical_and(earlier[None], mine[:, None, :]).astype(jnp.int32), axis=2
    )
    sel = jnp.logical_and(
        mine[:, None, :], before[:, None, :] == jnp.arange(MOST, dtype=jnp.int32)[None, :, None]
    )
    recv_pos = jnp.sum(jnp.where(sel, place[:, None, :] + 1, 0), axis=2).reshape(-1) - 1
    fill = recv_pos[None, :] == unit_index[:, None]
    slot_of = jnp.sum(jnp.where(fill, slot_index[None, :], 0), axis=1).astype(jnp.int32)
    pos_of = jnp.maximum(recv_pos, 0).astype(jnp.int32)

    kv_weight = lax.dynamic_slice_in_dim(w_keyval, kv_first * 2 * HEAD, kvcols, 1)
    ones = jnp.ones((HEAD,), jnp.float32)
    hgain = jnp.concatenate(
        [jnp.tile(query_gain, qcols // HEAD)]
        + [jnp.concatenate([key_gain, ones])] * kv_heads
    )[None, :]
    normed_cols = jnp.concatenate(
        [jnp.ones((qcols,), jnp.float32)]
        + [jnp.concatenate([ones, jnp.zeros((HEAD,), jnp.float32)])] * kv_heads
    )[None, :]
    lane = jnp.arange(LANES, dtype=jnp.int32)
    mean_mat = jnp.where(
        lane[:, None] // HEAD == lane[None, :] // HEAD, 1.0 / HEAD, 0.0
    ).astype(jnp.bfloat16)

    const = lambda shape: pl.BlockSpec(
        shape, lambda i: (0,) * len(shape), pipeline_mode=pl.Buffered(1)
    )
    packed = pl.pallas_call(
        functools.partial(qkv_kernel, unit_rows, slots),
        grid=(tokens // TILE,),
        in_specs=[
            SMEM,
            pl.BlockSpec((TILE, width), lambda i: (i, 0)),
            const((1, width)),
            const((width, qcols)),
            const((width, kvcols)),
            const((1, cols)),
            const((1, cols)),
            const((LANES, LANES)),
        ],
        out_specs=pl.BlockSpec((slots * unit_rows, cols), lambda i: (0, 0)),
        out_shape=jax.ShapeDtypeStruct((slots * unit_rows, cols), jnp.bfloat16),
        scratch_shapes=[pltpu.VMEM((tokens, cols), jnp.bfloat16)],
        compiler_params=params,
        name="qkv",
    )(src, full, attn_gain[None, :], w_query, kv_weight, hgain, normed_cols, mean_mat)

    received = lax.all_to_all(
        packed.reshape(groups, MOST * unit_rows, cols), "dp", split_axis=0, concat_axis=0, tiled=True
    ).reshape(slots * unit_rows, cols)

    starts = segment_starts(seg_ids[0])
    half = HEAD // 2
    inverse = THETA ** (-jnp.arange(half, dtype=jnp.float32) * 2.0 / HEAD)
    positions = jnp.arange(tokens, dtype=jnp.int32) - starts
    angles = positions.astype(jnp.float32)[:, None] * inverse[None, :]
    cosine, sine = jnp.cos(angles), jnp.sin(angles)
    cosq = jnp.tile(cosine, (1, 4))
    sinq = jnp.tile(sine, (1, 4))
    coskv = jnp.concatenate([cosine, cosine, jnp.ones((tokens, HEAD), jnp.float32)], axis=1)
    sinkv = jnp.concatenate([sine, sine, jnp.zeros((tokens, HEAD), jnp.float32)], axis=1)
    inn, out_l = lane[:, None], lane[None, :]
    rot = jnp.where(
        jnp.logical_and(out_l % HEAD < half, inn == out_l + half),
        -1.0,
        jnp.where(jnp.logical_and(out_l % HEAD >= half, inn == out_l - half), 1.0, 0.0),
    ).astype(jnp.bfloat16)

    npages = tokens // PAGE
    kv_pages, back = pl.pallas_call(
        functools.partial(attention_kernel, unit_rows, slots, qcols),
        in_specs=[SMEM] * 3 + [VMEM] * 7,
        out_specs=[VMEM] * 2,
        out_shape=[
            jax.ShapeDtypeStruct((npages, PAGE, kvcols), jnp.bfloat16),
            jax.ShapeDtypeStruct((slots * unit_rows, qcols), jnp.bfloat16),
        ],
        scratch_shapes=[
            pltpu.VMEM((tokens, cols), jnp.bfloat16),
            pltpu.VMEM((tokens, qcols), jnp.bfloat16),
            pltpu.VMEM((tokens, kvcols), jnp.bfloat16),
            pltpu.VMEM((tokens, qcols), jnp.bfloat16),
        ],
        compiler_params=params,
        name="attention",
    )(slot_of, pos_of, page_table[0], received, cosq, sinq, coskv, sinkv, starts[:, None], rot)

    if cache_cols < kvcols:
        offset = rank_t * cache_cols - kv_first * 2 * HEAD
        kv_pages = lax.dynamic_slice_in_dim(kv_pages, offset, cache_cols, 2)

    returned = lax.all_to_all(
        back.reshape(groups, MOST * unit_rows, qcols), "dp", split_axis=0, concat_axis=0, tiled=True
    ).reshape(slots * unit_rows, qcols)
    att = pl.pallas_call(
        functools.partial(gather_kernel, unit_rows),
        in_specs=[SMEM, VMEM],
        out_specs=VMEM,
        out_shape=jax.ShapeDtypeStruct((tokens, qcols), jnp.bfloat16),
        compiler_params=params,
        name="ungroup",
    )(slot, returned)
    att_full = lax.all_gather(att, "tensor", axis=1, tiled=True)

    ff = w_gate.shape[1]
    ft = next(t for t in (512, 256, 128) if ff % t == 0)
    dt = 512
    nf, nd = ff // ft, width // dt
    part, mid = pl.pallas_call(
        functools.partial(ffn_kernel, nf),
        grid=(nf + nd,),
        in_specs=[
            SMEM,
            const((tokens, width)),
            const((tokens, qcols * shards)),
            const((qcols * shards, width)),
            const((1, width)),
            pl.BlockSpec((width, ft), lambda i: (0, jnp.minimum(i, nf - 1))),
            pl.BlockSpec((width, ft), lambda i: (0, jnp.minimum(i, nf - 1))),
            pl.BlockSpec((ff, dt), lambda i: (0, jnp.maximum(i - nf, 0))),
        ],
        out_specs=[
            pl.BlockSpec((tokens, dt), lambda i: (0, jnp.maximum(i - nf, 0))),
            pl.BlockSpec((tokens, fp), lambda i: (0, 0)),
        ],
        out_shape=[
            jax.ShapeDtypeStruct((tokens, width), jnp.bfloat16),
            jax.ShapeDtypeStruct((tokens, fp), jnp.bfloat16),
        ],
        scratch_shapes=[
            pltpu.VMEM((tokens, width), jnp.bfloat16),
            pltpu.VMEM((tokens, ff), jnp.bfloat16),
        ],
        compiler_params=params,
        name="ffn",
    )(
        rank_t.astype(jnp.int32)[None], full, att_full, wo_full, ffn_gain[None, :],
        w_gate, w_up, w_down,
    )
    summed = lax.psum_scatter(part, "tensor", scatter_dimension=1, tiled=True)
    result = (mid.astype(jnp.float32) + summed.astype(jnp.float32)).astype(jnp.bfloat16)
    return (result, kv_pages)


def solution(mesh):
    return jax.shard_map(
        on_device,
        mesh=mesh,
        in_specs=(
            P("dp", "tensor"),
            P("dp", None),
            P("dp", None),
            P("dp", None),
            P(),
            P(None, "tensor"),
            P(),
            P(),
            P(),
            P("tensor", None),
            P(),
            P(None, "tensor"),
            P(None, "tensor"),
            P("tensor", None),
        ),
        out_specs=(P("dp", "tensor"), P("dp", None, "tensor")),
        check_vma=False,
    )
```

time: 326 us -> 231 us (0.71)
  matrix products: 85.6 us -> 0 us
  waiting for transfers between devices: 144 us -> 66.6 us
  Pallas kernels: 0 us -> 77.3 us
  blocking collectives: 0 us -> 30.7 us
  local copies, waits for them, and re-layouts: 37.2 us -> 8.48 us
  other arithmetic: 18.1 us -> 12.9 us
    dot_general x13 -> x0, matrix products: 85.6 us -> none  [the longest x1 33 us: on_device(): jnp.dot(hidden, w_down, preferred_element_type=jnp.float32)]
    pallas_call x0 -> x4, Pallas kernels: none -> 77.3 us  [the longest x1 53.9 us: on_device(): pl.pallas_call(functools.partial(ffn_kernel, nf), grid=(nf + nd,), in_spe...]
    all_to_all x3 -> x2, waiting for transfers between devices: 92.7 us -> 42 us  [the longest x1 21.5 us: on_device(): lax.all_to_all(back.reshape(groups, MOST * unit_rows, qcols), 'dp', split...]
    reshape x10 -> x0, local copies, waits for them, and re-layouts: 32 us -> none  [the longest x1 4.38 us: on_device(): packed.reshape(groups, MOST, width)]
    all_gather x0 -> x1, blocking collectives: none -> 30.7 us  [on_device(): deal_all = lax.all_gather(deal[0], 'dp', axis=0)]
    psum x1 -> x0, waiting for transfers between devices: 29.7 us -> none  [on_device(): lax.psum(jnp.dot(attended, w_out, preferred_element_type=jnp.float32).ast...]
    reduce_sum x5, other arithmetic: 9.04 us -> 2.04 us  [the longest x1 0.71 us: on_device(): jnp.sum(jnp.where(hot, unit_index[None, :], 0), axis=1).astype(jnp.int32)]
    all_to_all x3 -> x2, starting transfers between devices: 21.1 us -> 18.3 us  [the longest x1 14 us: on_device(): lax.all_to_all(packed.reshape(groups, MOST * unit_rows, cols), 'dp', spli...]
  transfers between devices with their start and end apart: 6 -> 6, of which waited for: 5 -> 4; matrix products, arithmetic and copies ran while one was open for 6% -> 6% of each run, Pallas kernels for 0% -> 10%
where the time goes in v1:
time: 231 us; the launch traced here: 229 us
  Pallas kernels  77.3 us (33%)
  waiting for transfers between devices  66.6 us (29%)
  blocking collectives  30.7 us (13%)
  starting transfers between devices  18.6 us (8%)
  between operations  14.6 us (6%)
  other arithmetic  12.9 us (6%)
  local copies, waits for them, and re-layouts  8.48 us (4%)
    pallas_call x1, Pallas kernels, on_device(): pl.pallas_call(functools.partial(ffn_kernel, nf), grid=(nf + nd,), in_spe...  53.9 us
    all_gather x1, blocking collectives, on_device(): deal_all = lax.all_gather(deal[0], 'dp', axis=0)  30.7 us
    all_to_all x1, waiting for transfers between devices, on_device(): lax.all_to_all(back.reshape(groups, MOST * unit_rows, qcols), 'dp', split...  21.5 us
    all_to_all x1, waiting for transfers between devices, on_device(): lax.all_to_all(packed.reshape(groups, MOST * unit_rows, cols), 'dp', spli...  20.5 us
    all_to_all x1, starting transfers between devices, on_device(): lax.all_to_all(packed.reshape(groups, MOST * unit_rows, cols), 'dp', spli...  14 us
    reduce_scatter x1, waiting for transfers between devices, on_device(): summed = lax.psum_scatter(part, 'tensor', scatter_dimension=1, tiled=True)  13.5 us
    pallas_call x1, Pallas kernels, on_device(): pl.pallas_call(functools.partial(attention_kernel, unit_rows, slots, qcol...  11.3 us
    all_gather x1, waiting for transfers between devices, on_device(): att_full = lax.all_gather(att, 'tensor', axis=1, tiled=True)  9.65 us
  transfers between devices with their start and end apart: 6, of which 4 were waited for; matrix products, arithmetic and copies ran while one was open for 6% of the time, Pallas kernels for 10%

profile of v1, /device:TPU:12, one launch (start us, length us, event | category | flops | bytes accessed | tf_op | source)
XLA Modules:
  0.0 229.0 jit_solution(7136417106491620802)
XLA Ops:
  7.3 0.7 all-gather.5.cloned.1.call-update
  8.0 0.7 all-gather.9.cloned.1.call-update
  8.8 0.5 slice.17
  9.3 0.2 convert_reduce_fusion.1
  9.5 0.7 select_reduce_fusion.src
  10.2 0.1 tile.13
  10.3 0.1 concatenate.16
  10.4 0.6 broadcast_in_dim.96.hgain
  11.0 30.7 %all-gather = s32[16,1,32]{2,1,0:T(1,128)S(1)} all-gather(s32[1,1,32]{2,1,0:T(1,128)S(1)} %bitcast.59), channel_id=1, replica_groups=mesh['dp'=16,'tensor'=2] {'dp'}, dimensions={0}, use_global_device_ids=true | all-gather | bytes 2176 | tf_op jit(solution)/shard_map/all_gather | solution.py:225
  41.6 0.7 select_convert_fusion.1.mean_mat
  43.0 1.1 constant_dynamic-slice_fusion.wkv
  44.1 9.5 %qkv.1 = bf16[1024,768]{1,0:T(8,128)(2,1)} custom-call(s32[32]{0:T(128)} %select_reduce_fusion.src, bf16[1024,2048]{1,0:T(8,128)(2,1)} %all-gather.5.cloned.1.call-done.x, f32[1,2048]{1,0:T(1,128)} %bitcast.57, bf16[2048,512]{1,0:T(8,128)(2,1)} %wq.1, bf16[2048,256]{1,0:T(8,128)(2,1)} %constant_dynamic-slice_fusion.wkv, f32[1,768]{1,0:T(1,128)} %broadcast_in_dim.96.hgain, ...), custom_call_target="tpu_custom_call" | custom-call | tf_op jit(solution)/shard_map/qkv/pallas_call | solution.py:269
  53.6 14.0 %all-to-all-start = ((bf16[16,64,768]{2,1,0:T(8,128)(2,1)}), bf16[16,64,768]{2,1,0:T(8,128)(2,1)S(1)}, u32[]{:S(2)}, u32[]{:S(2)}) async-start(bf16[16,64,768]{2,1,0:T(8,128)(2,1)} %bitcast.46), calls=%async_computation | async-start | bytes 3145728 | tf_op jit(solution)/shard_map/all_to_all | solution.py:289
  67.6 0.1 add_select_fusion.2
  67.7 0.1 pad.5.clone
  67.8 0.1 pad.2.clone
  67.9 0.3 reduce-window.9
  68.2 0.1 slice.20
  68.3 0.3 convert_reduce_fusion
  68.6 0.1 select_reduce_fusion.2
  68.7 0.1 copy.32
  68.8 0.1 sub.53
  68.9 0.1 slice_reduce_fusion
  69.0 0.1 fusion.8
  69.1 1.0 copy.38.starts
  70.1 1.9 multiply_sine_fusion
  72.0 0.2 copy.35
  72.2 0.2 copy.34
  72.4 0.1 tile.14
  72.4 1.0 copy.36.cosq
  73.5 1.0 copy.37.sinq
  74.5 0.7 select_reduce_fusion.1.slot_of
  75.2 0.5 broadcast_maximum_fusion.1.pos_of
  75.7 0.6 select_convert_fusion.rot
  76.3 1.3 maximum_maximum_fusion
  77.7 20.5 %all-to-all-done = bf16[16,64,768]{2,1,0:T(8,128)(2,1)S(1)} async-done(((bf16[16,64,768]{2,1,0:T(8,128)(2,1)}), bf16[16,64,768]{2,1,0:T(8,128)(2,1)S(1)}, u32[]{:S(2)}, u32[]{:S(2)}) %all-to-all-start) | async-done | bytes 1572896 | tf_op jit(solution)/shard_map/all_to_all | solution.py:289
  98.2 1.1 copy-done.2
  99.3 11.3 %attention.1 = (bf16[8,128,256]{2,1,0:T(8,128)(2,1)}, bf16[1024,512]{1,0:T(8,128)(2,1)}) custom-call(s32[32]{0:T(128)} %select_reduce_fusion.1.slot_of, s32[32]{0:T(128)} %broadcast_maximum_fusion.1.pos_of, s32[8]{0:T(128)} %bitcast.58, bf16[1024,768]{1,0:T(8,128)(2,1)} %bitcast.45, f32[1024,128]{1,0:T(8,128)} %copy.36.cosq, f32[1024,128]{1,0:T(8,128)} %copy.37.sinq, ...), custom_call_target="tpu_custom_call" | custom-call | tf_op jit(solution)/shard_map/attention/pallas_call | solution.py:311
  110.6 4.3 %all-to-all-start.1 = ((bf16[16,64,512]{2,1,0:T(8,128)(2,1)}), bf16[16,64,512]{2,1,0:T(8,128)(2,1)S(1)}, u32[]{:S(2)}, u32[]{:S(2)}) async-start(bf16[16,64,512]{2,1,0:T(8,128)(2,1)} %bitcast.50), calls=%async_computation.1 | async-start | bytes 2097152 | tf_op jit(solution)/shard_map/all_to_all | solution.py:333
  114.9 0.5 multiply_add_fusion.slot_of
  115.5 21.5 %all-to-all-done.1 = bf16[16,64,512]{2,1,0:T(8,128)(2,1)S(1)} async-done(((bf16[16,64,512]{2,1,0:T(8,128)(2,1)}), bf16[16,64,512]{2,1,0:T(8,128)(2,1)S(1)}, u32[]{:S(2)}, u32[]{:S(2)}) %all-to-all-start.1) | async-done | bytes 1048608 | tf_op jit(solution)/shard_map/all_to_all | solution.py:333
  137.0 1.0 copy-done.3
  138.0 2.5 %ungroup.1 = bf16[1024,512]{1,0:T(8,128)(2,1)} custom-call(s32[32]{0:T(128)} %multiply_add_fusion.slot_of, bf16[1024,512]{1,0:T(8,128)(2,1)} %bitcast.47), custom_call_target="tpu_custom_call" | custom-call | tf_op jit(solution)/shard_map/ungroup/pallas_call | solution.py:336
  140.5 0.2 reduce-scatter.2.cloned.1.call-start
  140.8 9.7 %all-gather.7.cloned.1.call-done.att = bf16[1024,1024]{1,0:T(8,128)(2,1)} async-done(((bf16[1024,512]{1,0:T(8,128)(2,1)}), bf16[1024,1024]{1,0:T(8,128)(2,1)}) %all-gather.7.cloned.1.call-update) | async-done | bytes 2097168 | tf_op jit(solution)/shard_map/all_gather | solution.py:344
  150.4 53.9 %ffn.1 = (bf16[1024,2048]{1,0:T(8,128)(2,1)}, bf16[1024,1024]{1,0:T(8,128)(2,1)}) custom-call(s32[1]{0:T(128)} %bitcast.rank, bf16[1024,2048]{1,0:T(8,128)(2,1)} %all-gather.5.cloned.1.call-done.x, bf16[1024,1024]{1,0:T(8,128)(2,1)} %all-gather.7.cloned.1.call-done.att, bf16[1024,2048]{1,0:T(8,128)(2,1)} %all-gather.9.cloned.1.call-done.wo, ...), custom_call_target="tpu_custom_call" | custom-call | tf_op jit(solution)/shard_map/ffn/pallas_call | solution.py:350
  204.3 13.5 %reduce-scatter.2.cloned.1.call-done = bf16[1024,1024]{1,0:T(8,128)(2,1)} async-done(((bf16[1024,2048]{1,0:T(8,128)(2,1)}), bf16[1024,1024]{1,0:T(8,128)(2,1)}) %reduce-scatter.2.cloned.1.call-update) | async-done | bytes 2097168 | tf_op jit(solution)/shard_map/reduce_scatter | solution.py:381
  217.8 4.7 %add_convert_fusion = bf16[1024,1024]{1,0:T(8,128)(2,1)} fusion(bf16[1024,1024]{1,0:T(8,128)(2,1)} %reduce-scatter.2.cloned.1.call-done, bf16[1024,1024]{1,0:T(8,128)(2,1)} %get-tuple-element.7), kind=kLoop, calls=%fused_computation | loop fusion | flops 4194304 | bytes 6291456 | tf_op jit(solution)/shard_map/convert_element_type | solution.py:382
  (37 shorter events, 0.4 us)
Async XLA Ops:
  7.2 35.8 %copy-start = (bf16[2048,512]{1,0:T(8,128)(2,1)S(1)}, bf16[2048,512]{1,0:T(8,128)(2,1)}, u32[]{:S(2)}) copy-start(bf16[2048,512]{1,0:T(8,128)(2,1)} %param.20) | copy-start | bytes 6291460
  7.2 1.5 copy-start.7
  7.2 1.6 copy-start.4
  7.2 3.0 %copy-start.6 = (f32[64]{0:T(128)S(1)}, f32[64]{0:T(128)}, u32[]{:S(2)}) copy-start(f32[64]{0:T(128)} %param.21) | copy-start | bytes 772
  7.2 3.1 %copy-start.5 = (f32[64]{0:T(128)S(1)}, f32[64]{0:T(128)}, u32[]{:S(2)}) copy-start(f32[64]{0:T(128)} %param.22) | copy-start | bytes 772
  7.2 36.9 %all-gather.5.cloned.1.call-start = ((), (), s32[]{:S(2)}) async-start(), calls=%async_computation.3 | async-start | bytes 6291456 | tf_op jit(solution)/shard_map/all_gather | solution.py:224
  8.0 132.8 %all-gather.9.cloned.1.call-start = ((), (), s32[]{:S(2)}) async-start(), calls=%async_computation.5 | async-start | bytes 6291456 | tf_op jit(solution)/shard_map/all_gather | solution.py:226
  53.6 44.5 %all-to-all-start = ((bf16[16,64,768]{2,1,0:T(8,128)(2,1)}), bf16[16,64,768]{2,1,0:T(8,128)(2,1)S(1)}, u32[]{:S(2)}, u32[]{:S(2)}) async-start(bf16[16,64,768]{2,1,0:T(8,128)(2,1)} %bitcast.46), calls=%async_computation | async-start | bytes 3145728 | tf_op jit(solution)/shard_map/all_to_all | solution.py:289
  98.1 1.1 copy-start.2
  110.6 26.4 %all-to-all-start.1 = ((bf16[16,64,512]{2,1,0:T(8,128)(2,1)}), bf16[16,64,512]{2,1,0:T(8,128)(2,1)S(1)}, u32[]{:S(2)}, u32[]{:S(2)}) async-start(bf16[16,64,512]{2,1,0:T(8,128)(2,1)} %bitcast.50), calls=%async_computation.1 | async-start | bytes 2097152 | tf_op jit(solution)/shard_map/all_to_all | solution.py:333
  114.9 35.5 %all-gather.7.cloned.1.call-start = ((), (), s32[]{:S(2)}) async-start(), calls=%async_computation.4 | async-start | bytes 3145728 | tf_op jit(solution)/shard_map/all_gather | solution.py:344
  137.0 1.0 copy-start.3
  140.5 77.3 %reduce-scatter.2.cloned.1.call-start = ((), (), s32[]{:S(2)}) async-start(), calls=%async_computation.6 | async-start | bytes 6291456 | tf_op jit(solution)/shard_map/reduce_scatter | solution.py:381
  217.8 4.7 %copy-start.1 = (bf16[2048,512]{1,0:T(8,128)(2,1)S(1)}, bf16[2048,512]{1,0:T(8,128)(2,1)}, u32[]{:S(2)}) copy-start(bf16[2048,512]{1,0:T(8,128)(2,1)} %param.20) | copy-start | bytes 6291460
Sparse Core Ops, SparseCore 0:
  9.6 15.0 all-gather.4
  26.3 14.8 all-gather.8
  140.6 9.7 all-gather.6
  204.5 13.3 reduce-scatter.1

commit v2 on v1

--- a/solution.py
+++ b/solution.py
@@ -17,9 +17,12 @@
 THETA = 10000.0
 LANES = 128
 TILE = 256
+ROWS = 512
+MESH = pl.DeviceIdType.MESH
 VMEM_LIMIT = 60 * 1024 * 1024
 
 VMEM = pl.BlockSpec(memory_space=pltpu.VMEM)
+ANY = pl.BlockSpec(memory_space=pl.ANY)
 SMEM = pl.BlockSpec(memory_space=pltpu.SMEM)
 
 
@@ -31,38 +34,110 @@
     return lax.cummax(marks, axis=0)
 
 
-def qkv_kernel(unit_rows, slots, src, x, gain, wq, wkv, hgain, normed_cols, mean_mat, out, held):
-    step = pl.program_id(0)
-    rows = x.shape[0]
-    qcols = wq.shape[1]
-    cols = qcols + wkv.shape[1]
-    xv = x[...].astype(jnp.float32)
-    ms = jnp.mean(xv * xv, axis=-1, keepdims=True)
-    xn = (xv * lax.rsqrt(ms + EPS) * gain[...]).astype(jnp.bfloat16)
-    q = jnp.dot(xn, wq[...], preferred_element_type=jnp.float32)
-    kv = jnp.dot(xn, wkv[...], preferred_element_type=jnp.float32)
-    here = pl.ds(pl.multiple_of(step * rows, rows), rows)
-    for first in range(0, cols, LANES):
-        if first < qcols:
-            part = q[:, first : first + LANES]
-        else:
-            part = kv[:, first - qcols : first - qcols + LANES]
-        mean = jnp.dot(
-            (part * part).astype(jnp.bfloat16), mean_mat[...], preferred_element_type=jnp.float32
+def greet(peers):
+    barrier = pltpu.get_barrier_semaphore()
+    for peer in peers:
+        pl.semaphore_signal(barrier, inc=1, device_id=peer, device_id_type=MESH)
+    pl.semaphore_wait(barrier, len(peers))
+
+
+def qkv_kernel(
+    groups, shards, pos, x, gain, wq_hbm, wkv_hbm, hgain, normed_cols,
+    mean_mat, held, xg, rpos, xn, wq, wkv, wsem, lsem, xsend, xrecv, psend, precv
+):
+    me, rank = lax.axis_index("dp"), lax.axis_index("tensor")
+    tokens, fp = x.shape
+    qcols, kvcols = wq.shape[1], wkv.shape[1]
+    cols = qcols + kvcols
+    chunks = tokens // TILE
+    kv_at = pl.multiple_of((rank * KVH // shards) * 2 * HEAD, 2 * HEAD)
+    loads = [
+        pltpu.make_async_copy(wq_hbm, wq, wsem.at[0]),
+        pltpu.make_async_copy(wkv_hbm.at[:, pl.ds(kv_at, kvcols)], wkv, wsem.at[1]),
+    ]
+    local = [
+        pltpu.make_async_copy(
+            x.at[c * TILE : (c + 1) * TILE, :],
+            xg.at[rank, c * TILE : (c + 1) * TILE, :],
+            lsem.at[c],
         )
-        at = slice(first, first + LANES)
-        scaled = part * lax.rsqrt(mean + EPS) * hgain[:, at]
-        held[here, at] = jnp.where(normed_cols[:, at] > 0.5, scaled, part).astype(jnp.bfloat16)
-
-    @pl.when(step == pl.num_programs(0) - 1)
-    def _():
-        def move(slot, carry):
-            frm = pl.multiple_of(src[slot] * unit_rows, unit_rows)
-            to = pl.multiple_of(slot * unit_rows, unit_rows)
-            out[pl.ds(to, unit_rows), :] = held[pl.ds(frm, unit_rows), :]
-            return carry
-
-        lax.fori_loop(0, slots, move, 0)
+        for c in range(chunks)
+    ]
+    for copy in local + loads:
+        copy.start()
+    greet(
+        [{"dp": lax.rem(me + d, groups)} for d in range(1, groups)]
+        + [{"tensor": lax.rem(rank + d, shards)} for d in range(1, shards)]
+    )
+    swaps = [
+        [
+            pltpu.make_async_remote_copy(
+                src_ref=x.at[c * TILE : (c + 1) * TILE, :],
+                dst_ref=xg.at[rank, c * TILE : (c + 1) * TILE, :],
+                send_sem=xsend.at[d - 1, c],
+                recv_sem=xrecv.at[d - 1, c],
+                device_id={"tensor": lax.rem(rank + d, shards)},
+                device_id_type=MESH,
+            )
+            for d in range(1, shards)
+        ]
+        for c in range(chunks)
+    ]
+    for row in swaps:
+        for copy in row:
+            copy.start()
+    places = []
+    for d in range(1, groups):
+        to = lax.rem(me + d, groups)
+        places.append(
+            pltpu.make_async_remote_copy(
+                src_ref=pos.at[to],
+                dst_ref=rpos.at[me],
+                send_sem=psend.at[d - 1],
+                recv_sem=precv.at[d - 1],
+                device_id={"dp": to},
+                device_id_type=MESH,
+            )
+        )
+    for copy in places:
+        copy.start()
+    rpos[me] = pos[me]
+    for c in range(chunks):
+        here = slice(c * TILE, (c + 1) * TILE)
+        local[c].wait()
+        for copy in swaps[c]:
+            copy.wait_recv()
+        total = jnp.zeros((TILE, 1), jnp.float32)
+        for t in range(shards):
+            xv = xg[t, here, :].astype(jnp.float32)
+            total += jnp.sum(xv * xv, axis=-1, keepdims=True)
+        inv = lax.rsqrt(total / (fp * shards) + EPS)
+        for t in range(shards):
+            at = slice(t * fp, (t + 1) * fp)
+            xv = xg[t, here, :].astype(jnp.float32)
+            xn[:, at] = (xv * inv * gain[:, at]).astype(jnp.bfloat16)
+        if c == 0:
+            for copy in loads:
+                copy.wait()
+        q = jnp.dot(xn[...], wq[...], preferred_element_type=jnp.float32)
+        kv = jnp.dot(xn[...], wkv[...], preferred_element_type=jnp.float32)
+        for first in range(0, cols, LANES):
+            if first < qcols:
+                part = q[:, first : first + LANES]
+            else:
+                part = kv[:, first - qcols : first - qcols + LANES]
+            mean = jnp.dot(
+                (part * part).astype(jnp.bfloat16), mean_mat[...], preferred_element_type=jnp.float32
+            )
+            at = slice(first, first + LANES)
+            scaled = part * lax.rsqrt(mean + EPS) * hgain[:, at]
+            held[here, at] = jnp.where(normed_cols[:, at] > 0.5, scaled, part).astype(jnp.bfloat16)
+
+    for row in swaps:
+        for copy in row:
+            copy.wait_send()
+    for copy in places:
+        copy.wait()
 
 
 def attention_kernel(
@@ -140,64 +215,155 @@
     lax.fori_loop(0, slots, give, 0)
 
 
-def gather_kernel(unit_rows, slot_of, came, out):
-    def fetch(unit, carry):
-        frm = pl.multiple_of(slot_of[unit] * unit_rows, unit_rows)
+def move_kernel(unit_rows, source_of, came, out):
+    def move(unit, carry):
+        frm = pl.multiple_of(source_of[unit] * unit_rows, unit_rows)
         to = pl.multiple_of(unit * unit_rows, unit_rows)
         out[pl.ds(to, unit_rows), :] = came[pl.ds(frm, unit_rows), :]
         return carry
 
-    lax.fori_loop(0, out.shape[0] // unit_rows, fetch, 0)
+    lax.fori_loop(0, out.shape[0] // unit_rows, move, 0)
+
+
+def move_units(source_of, came, units, unit_rows):
+    return pl.pallas_call(
+        functools.partial(move_kernel, unit_rows),
+        in_specs=[SMEM, VMEM],
+        out_specs=VMEM,
+        out_shape=jax.ShapeDtypeStruct((units * unit_rows, came.shape[1]), came.dtype),
+        compiler_params=pltpu.CompilerParams(vmem_limit_bytes=VMEM_LIMIT),
+        name="move_units",
+    )(source_of, came)
 
 
 def ffn_kernel(
-    nf, rank, x, att, wo, gain, wg, wu, wd, part, mid, ffn_in, hidden
+    nf, shards, xg, came, wo, gain, wg, wu, wd_hbm, out, att, mid, ffn_in,
+    hidden, wd, sbuf, rbuf, wsem, asend, arecv, csend, crecv
 ):
     step = pl.program_id(0)
-    tokens = x.shape[0]
-    fp = mid.shape[1]
+    rank = lax.axis_index("tensor")
+    tokens, fp = mid.shape
+    qcols = came.shape[1]
     ft = wg.shape[1]
+    dt = wd.shape[2]
+    per = fp // dt
+    nd = per * shards
+    chunks = tokens // TILE
+
+    loads = []
+    for d in range(nd):
+        column = lax.rem(rank + 1 + d // per, shards) * fp + (d % per) * dt
+        loads.append(
+            pltpu.make_async_copy(
+                wd_hbm.at[:, pl.ds(pl.multiple_of(column, dt), dt)], wd.at[d], wsem.at[d]
+            )
+        )
+    swaps = [
+        [
+            pltpu.make_async_remote_copy(
+                src_ref=att.at[rank, c * TILE : (c + 1) * TILE, :],
+                dst_ref=att.at[rank, c * TILE : (c + 1) * TILE, :],
+                send_sem=asend.at[d - 1, c],
+                recv_sem=arecv.at[d - 1, c],
+                device_id={"tensor": lax.rem(rank + d, shards)},
+                device_id_type=MESH,
+            )
+            for d in range(1, shards)
+        ]
+        for c in range(chunks)
+    ]
+    shares = [
+        pltpu.make_async_remote_copy(
+            src_ref=sbuf.at[d],
+            dst_ref=rbuf.at[d],
+            send_sem=csend.at[d],
+            recv_sem=crecv.at[d],
+            device_id={"tensor": lax.rem(rank + 1 + d // per, shards)},
+            device_id_type=MESH,
+        )
+        for d in range(nd - per)
+    ]
 
     @pl.when(step == 0)
     def _():
-        own = pl.ds(pl.multiple_of(rank[0] * fp, fp), fp)
-
-        def rows(i, carry):
-            at = pl.ds(pl.multiple_of(i * TILE, TILE), TILE)
-            total = jnp.dot(att[at, :], wo[...], preferred_element_type=jnp.float32)
-            middle = (x[at, :].astype(jnp.float32) + total).astype(jnp.bfloat16)
-            ffn_in[at, :] = middle
-            mid[at, :] = ffn_in[at, own]
-            m = middle.astype(jnp.float32)
-            ms = jnp.mean(m * m, axis=-1, keepdims=True)
-            ffn_in[at, :] = (m * lax.rsqrt(ms + EPS) * gain[...]).astype(jnp.bfloat16)
-            return carry
-
-        lax.fori_loop(0, tokens // TILE, rows, 0)
+        greet([{"tensor": lax.rem(rank + d, shards)} for d in range(1, shards)])
+        for c in range(chunks):
+            here = slice(c * TILE, (c + 1) * TILE)
+            att[rank, here, :] = came[here, :]
+            for copy in swaps[c]:
+                copy.start()
+        for copy in loads:
+            copy.start()
+        for c in range(chunks):
+            here = slice(c * TILE, (c + 1) * TILE)
+            for copy in swaps[c]:
+                copy.wait_recv()
+            total = jnp.dot(
+                att[0, here, :], wo[0:qcols, :], preferred_element_type=jnp.float32
+            )
+            for t in range(1, shards):
+                total += jnp.dot(
+                    att[t, here, :],
+                    wo[t * qcols : (t + 1) * qcols, :],
+                    preferred_element_type=jnp.float32,
+                )
+            square = jnp.zeros((TILE, 1), jnp.float32)
+            for t in range(shards):
+                at = slice(t * fp, (t + 1) * fp)
+                m = (xg[t, here, :].astype(jnp.float32) + total[:, at]).astype(jnp.bfloat16)
+                ffn_in[here, at] = m
+                m = m.astype(jnp.float32)
+                square += jnp.sum(m * m, axis=-1, keepdims=True)
+            mid[here, :] = ffn_in[here, pl.ds(pl.multiple_of(rank * fp, fp), fp)]
+            inv = lax.rsqrt(square / (fp * shards) + EPS)
+            for t in range(shards):
+                at = slice(t * fp, (t + 1) * fp)
+                m = ffn_in[here, at].astype(jnp.float32)
+                ffn_in[here, at] = (m * inv * gain[:, at]).astype(jnp.bfloat16)
+        for row in swaps:
+            for copy in row:
+                copy.wait_send()
 
     @pl.when(step < nf)
     def _():
         cols = pl.ds(pl.multiple_of(step * ft, ft), ft)
 
         def rows(i, carry):
-            at = pl.ds(pl.multiple_of(i * TILE, TILE), TILE)
+            at = pl.ds(pl.multiple_of(i * ROWS, ROWS), ROWS)
             g = jnp.dot(ffn_in[at, :], wg[...], preferred_element_type=jnp.float32)
             u = jnp.dot(ffn_in[at, :], wu[...], preferred_element_type=jnp.float32)
             hidden[at, cols] = (g / (1.0 + jnp.exp(-g)) * u).astype(jnp.bfloat16)
             return carry
 
-        lax.fori_loop(0, tokens // TILE, rows, 0)
-
-    @pl.when(step >= nf)
-    def _():
-        def rows(i, carry):
-            at = pl.ds(pl.multiple_of(i * TILE, TILE), TILE)
-            part[at, :] = jnp.dot(
-                hidden[at, :], wd[...], preferred_element_type=jnp.float32
-            ).astype(jnp.bfloat16)
-            return carry
-
-        lax.fori_loop(0, tokens // TILE, rows, 0)
+        lax.fori_loop(0, tokens // ROWS, rows, 0)
+
+    for d in range(nd):
+        @pl.when(step == nf + d)
+        def _(d=d):
+            loads[d].wait()
+            j = d - (nd - per)
+            cols = slice(j * dt, (j + 1) * dt)
+            if j >= 0:
+                for k in range(shards - 1):
+                    shares[k * per + j].wait_recv()
+
+            def rows(i, carry):
+                at = pl.ds(pl.multiple_of(i * ROWS, ROWS), ROWS)
+                part = jnp.dot(hidden[at, :], wd[d], preferred_element_type=jnp.float32)
+                if j < 0:
+                    sbuf[d, at, :] = part.astype(jnp.bfloat16)
+                else:
+                    for k in range(shards - 1):
+                        part += rbuf[k * per + j, at, :].astype(jnp.float32)
+                    out[at, cols] = (mid[at, cols].astype(jnp.float32) + part).astype(jnp.bfloat16)
+                return carry
+
+            lax.fori_loop(0, tokens // ROWS, rows, 0)
+            if j < 0:
+                shares[d].start()
+            if d == nd - 1:
+                for copy in shares:
+                    copy.wait_send()
 
 
 def on_device(
@@ -221,8 +387,6 @@
     cols = qcols + kvcols
     params = pltpu.CompilerParams(vmem_limit_bytes=VMEM_LIMIT)
 
-    full = lax.all_gather(arrivals, "tensor", axis=1, tiled=True)
-    deal_all = lax.all_gather(deal[0], "dp", axis=0)
     wo_full = lax.all_gather(w_out, "tensor", axis=0, tiled=True)
 
     dest_row = deal[0]
@@ -235,20 +399,12 @@
     hot = slot[None, :] == slot_index[:, None]
     src = jnp.sum(jnp.where(hot, unit_index[None, :], 0), axis=1).astype(jnp.int32)
 
-    mine = deal_all // units == me
-    place = deal_all % units
-    before = jnp.sum(
-        jnp.logical_and(earlier[None], mine[:, None, :]).astype(jnp.int32), axis=2
+    slot_pos = jnp.sum(jnp.where(hot, dest_row[None, :] % units + 1, 0), axis=1) - 1
+    pos = jnp.broadcast_to(
+        jnp.pad(slot_pos.astype(jnp.int32).reshape(groups, 1, MOST), ((0, 0), (0, 0), (0, LANES - MOST))),
+        (groups, 8, LANES),
     )
-    sel = jnp.logical_and(
-        mine[:, None, :], before[:, None, :] == jnp.arange(MOST, dtype=jnp.int32)[None, :, None]
-    )
-    recv_pos = jnp.sum(jnp.where(sel, place[:, None, :] + 1, 0), axis=2).reshape(-1) - 1
-    fill = recv_pos[None, :] == unit_index[:, None]
-    slot_of = jnp.sum(jnp.where(fill, slot_index[None, :], 0), axis=1).astype(jnp.int32)
-    pos_of = jnp.maximum(recv_pos, 0).astype(jnp.int32)
-
-    kv_weight = lax.dynamic_slice_in_dim(w_keyval, kv_first * 2 * HEAD, kvcols, 1)
+
     ones = jnp.ones((HEAD,), jnp.float32)
     hgain = jnp.concatenate(
         [jnp.tile(query_gain, qcols // HEAD)]
@@ -266,25 +422,38 @@
     const = lambda shape: pl.BlockSpec(
         shape, lambda i: (0,) * len(shape), pipeline_mode=pl.Buffered(1)
     )
-    packed = pl.pallas_call(
-        functools.partial(qkv_kernel, unit_rows, slots),
-        grid=(tokens // TILE,),
-        in_specs=[
-            SMEM,
-            pl.BlockSpec((TILE, width), lambda i: (i, 0)),
-            const((1, width)),
-            const((width, qcols)),
-            const((width, kvcols)),
-            const((1, cols)),
-            const((1, cols)),
-            const((LANES, LANES)),
+    held, xg, rpos = pl.pallas_call(
+        functools.partial(qkv_kernel, groups, shards),
+        in_specs=[VMEM, ANY, VMEM, ANY, ANY, VMEM, VMEM, VMEM],
+        out_specs=[VMEM] * 3,
+        out_shape=[
+            jax.ShapeDtypeStruct((tokens, cols), jnp.bfloat16),
+            jax.ShapeDtypeStruct((shards, tokens, fp), jnp.bfloat16),
+            jax.ShapeDtypeStruct((groups, 8, LANES), jnp.int32),
         ],
-        out_specs=pl.BlockSpec((slots * unit_rows, cols), lambda i: (0, 0)),
-        out_shape=jax.ShapeDtypeStruct((slots * unit_rows, cols), jnp.bfloat16),
-        scratch_shapes=[pltpu.VMEM((tokens, cols), jnp.bfloat16)],
-        compiler_params=params,
+        scratch_shapes=[
+            pltpu.VMEM((TILE, width), jnp.bfloat16),
+            pltpu.VMEM((width, qcols), jnp.bfloat16),
+            pltpu.VMEM((width, kvcols), jnp.bfloat16),
+            pltpu.SemaphoreType.DMA((2,)),
+            pltpu.SemaphoreType.DMA((tokens // TILE,)),
+            pltpu.SemaphoreType.DMA((shards - 1, tokens // TILE)),
+            pltpu.SemaphoreType.DMA((shards - 1, tokens // TILE)),
+            pltpu.SemaphoreType.DMA((groups - 1,)),
+            pltpu.SemaphoreType.DMA((groups - 1,)),
+        ],
+        compiler_params=pltpu.CompilerParams(
+            vmem_limit_bytes=VMEM_LIMIT, collective_id=0, has_side_effects=True
+        ),
         name="qkv",
-    )(src, full, attn_gain[None, :], w_query, kv_weight, hgain, normed_cols, mean_mat)
+    )(pos, arrivals, attn_gain[None, :], w_query, w_keyval, hgain, normed_cols, mean_mat)
+
+    packed = move_units(src, held, slots, unit_rows)
+
+    recv_pos = rpos[:, 0, :MOST].reshape(-1)
+    fill = recv_pos[None, :] == unit_index[:, None]
+    slot_of = jnp.sum(jnp.where(fill, slot_index[None, :], 0), axis=1).astype(jnp.int32)
+    pos_of = jnp.maximum(recv_pos, 0).astype(jnp.int32)
 
     received = lax.all_to_all(
         packed.reshape(groups, MOST * unit_rows, cols), "dp", split_axis=0, concat_axis=0, tiled=True
@@ -333,53 +502,47 @@
     returned = lax.all_to_all(
         back.reshape(groups, MOST * unit_rows, qcols), "dp", split_axis=0, concat_axis=0, tiled=True
     ).reshape(slots * unit_rows, qcols)
-    att = pl.pallas_call(
-        functools.partial(gather_kernel, unit_rows),
-        in_specs=[SMEM, VMEM],
-        out_specs=VMEM,
-        out_shape=jax.ShapeDtypeStruct((tokens, qcols), jnp.bfloat16),
-        compiler_params=params,
-        name="ungroup",
-    )(slot, returned)
-    att_full = lax.all_gather(att, "tensor", axis=1, tiled=True)
+    own_att = move_units(slot, returned, units, unit_rows)
 
     ff = w_gate.shape[1]
     ft = next(t for t in (512, 256, 128) if ff % t == 0)
-    dt = 512
-    nf, nd = ff // ft, width // dt
-    part, mid = pl.pallas_call(
-        functools.partial(ffn_kernel, nf),
+    nf = ff // ft
+    dt = min(512, fp)
+    nd = width // dt
+    away = nd - fp // dt
+    result = pl.pallas_call(
+        functools.partial(ffn_kernel, nf, shards),
         grid=(nf + nd,),
         in_specs=[
-            SMEM,
-            const((tokens, width)),
-            const((tokens, qcols * shards)),
+            const((shards, tokens, fp)),
+            const((tokens, qcols)),
             const((qcols * shards, width)),
             const((1, width)),
             pl.BlockSpec((width, ft), lambda i: (0, jnp.minimum(i, nf - 1))),
             pl.BlockSpec((width, ft), lambda i: (0, jnp.minimum(i, nf - 1))),
-            pl.BlockSpec((ff, dt), lambda i: (0, jnp.maximum(i - nf, 0))),
+            ANY,
         ],
-        out_specs=[
-            pl.BlockSpec((tokens, dt), lambda i: (0, jnp.maximum(i - nf, 0))),
-            pl.BlockSpec((tokens, fp), lambda i: (0, 0)),
-        ],
-        out_shape=[
-            jax.ShapeDtypeStruct((tokens, width), jnp.bfloat16),
-            jax.ShapeDtypeStruct((tokens, fp), jnp.bfloat16),
-        ],
+        out_specs=pl.BlockSpec((tokens, fp), lambda i: (0, 0), pipeline_mode=pl.Buffered(1)),
+        out_shape=jax.ShapeDtypeStruct((tokens, fp), jnp.bfloat16),
         scratch_shapes=[
+            pltpu.VMEM((shards, tokens, qcols), jnp.bfloat16),
+            pltpu.VMEM((tokens, fp), jnp.bfloat16),
             pltpu.VMEM((tokens, width), jnp.bfloat16),
             pltpu.VMEM((tokens, ff), jnp.bfloat16),
+            pltpu.VMEM((nd, ff, dt), jnp.bfloat16),
+            pltpu.VMEM((away, tokens, dt), jnp.bfloat16),
+            pltpu.VMEM((away, tokens, dt), jnp.bfloat16),
+            pltpu.SemaphoreType.DMA((nd,)),
+            pltpu.SemaphoreType.DMA((shards - 1, tokens // TILE)),
+            pltpu.SemaphoreType.DMA((shards - 1, tokens // TILE)),
+            pltpu.SemaphoreType.DMA((away,)),
+            pltpu.SemaphoreType.DMA((away,)),
         ],
-        compiler_params=params,
+        compiler_params=pltpu.CompilerParams(
+            vmem_limit_bytes=VMEM_LIMIT, collective_id=1, has_side_effects=True
+        ),
         name="ffn",
-    )(
-        rank_t.astype(jnp.int32)[None], full, att_full, wo_full, ffn_gain[None, :],
-        w_gate, w_up, w_down,
-    )
-    summed = lax.psum_scatter(part, "tensor", scatter_dimension=1, tiled=True)
-    result = (mid.astype(jnp.float32) + summed.astype(jnp.float32)).astype(jnp.bfloat16)
+    )(xg, own_att, wo_full, ffn_gain[None, :], w_gate, w_up, w_down)
     return (result, kv_pages)
 
 

time: 231 us -> 185 us (0.80)
  blocking collectives: 30.7 us -> 0 us
  waiting for transfers between devices: 66.6 us -> 51.2 us
  starting transfers between devices: 18.6 us -> 12.4 us
  Pallas kernels: 77.3 us -> 83.3 us
  local copies, waits for them, and re-layouts: 8.48 us -> 13.3 us
  other arithmetic: 12.9 us -> 9.01 us
    all_gather x1 -> x0, blocking collectives: 30.7 us -> none  [on_device(): deal_all = lax.all_gather(deal[0], 'dp', axis=0)]
    reduce_scatter x1 -> x0, waiting for transfers between devices: 13.5 us -> none  [on_device(): summed = lax.psum_scatter(part, 'tensor', scatter_dimension=1, tiled=True)]
    all_gather x2 -> x0, waiting for transfers between devices: 9.65 us -> none  [the longest x1 9.65 us: on_device(): att_full = lax.all_gather(att, 'tensor', axis=1, tiled=True)]
    all_to_all x1, starting transfers between devices: 14 us -> 6.02 us  [on_device(): lax.all_to_all(packed.reshape(groups, MOST * unit_rows, cols), 'dp', spli...]
    pallas_call x3 -> x4, Pallas kernels: 65.9 us -> 72 us  [the longest x1 51.4 us: on_device(): pl.pallas_call(functools.partial(ffn_kernel, nf, shards), grid=(nf + nd,)...]
    all_to_all x1, waiting for transfers between devices: 20.5 us -> 25.7 us  [on_device(): lax.all_to_all(packed.reshape(groups, MOST * unit_rows, cols), 'dp', spli...]
    convert_element_type x1 -> x0, other arithmetic: 4.65 us -> none  [on_device(): (mid.astype(jnp.float32) + summed.astype(jnp.float32)).astype(jnp.bfloat16)]
    all_to_all x1, waiting for transfers between devices: 21.5 us -> 25 us  [on_device(): lax.all_to_all(back.reshape(groups, MOST * unit_rows, qcols), 'dp', split...]
  transfers between devices with their start and end apart: 6 -> 3, of which waited for: 4 -> 2; matrix products, arithmetic and copies ran while one was open for 6% -> 6% of each run, Pallas kernels for 10% -> 7%
where the time goes in v2:
time: 185 us; the launch traced here: 184 us
  Pallas kernels  83.3 us (45%)
  waiting for transfers between devices  51.2 us (28%)
  between operations  14.8 us (8%)
  local copies, waits for them, and re-layouts  13.3 us (7%)
  starting transfers between devices  12.4 us (7%)
  other arithmetic  9.01 us (5%)
    pallas_call x1, Pallas kernels, on_device(): pl.pallas_call(functools.partial(ffn_kernel, nf, shards), grid=(nf + nd,)...  51.4 us
    all_to_all x1, waiting for transfers between devices, on_device(): lax.all_to_all(packed.reshape(groups, MOST * unit_rows, cols), 'dp', spli...  25.7 us
    all_to_all x1, waiting for transfers between devices, on_device(): lax.all_to_all(back.reshape(groups, MOST * unit_rows, qcols), 'dp', split...  25 us
    pallas_call x1, Pallas kernels, on_device(): pl.pallas_call(functools.partial(qkv_kernel, groups, shards), in_specs=[V...  15.3 us
    pallas_call x1, Pallas kernels, on_device(): pl.pallas_call(functools.partial(attention_kernel, unit_rows, slots, qcol...  11.3 us
    all_to_all x1, starting transfers between devices, on_device(): lax.all_to_all(back.reshape(groups, MOST * unit_rows, qcols), 'dp', split...  6.16 us
    all_to_all x1, starting transfers between devices, on_device(): lax.all_to_all(packed.reshape(groups, MOST * unit_rows, cols), 'dp', spli...  6.02 us
    pallas_call x2, Pallas kernels, move_units(): pl.pallas_call(functools.partial(move_kernel, unit_rows), in_specs=[SMEM,...  5.33 us
  transfers between devices with their start and end apart: 3, of which 2 were waited for; matrix products, arithmetic and copies ran while one was open for 6% of the time, Pallas kernels for 7%

profile of v2, /device:TPU:12, one launch (start us, length us, event | category | flops | bytes accessed | tf_op | source)
XLA Modules:
  0.0 184.0 jit_solution(6374752495898407784)
XLA Ops:
  7.2 0.7 fusion.6
  7.8 0.7 and_select_fusion.3
  8.5 0.2 convert_reduce_fusion
  8.7 0.6 select_reduce_fusion
  9.3 0.1 sub.42
  9.4 0.7 tile.12
  10.1 0.1 tile.13
  10.2 0.8 concatenate.16
  11.0 0.6 broadcast_in_dim.90.hgain
  11.6 0.7 select_convert_fusion.1.mean_mat
  12.3 0.6 broadcast_in_dim.87.pos
  12.9 15.3 %qkv.1 = (bf16[1024,768]{1,0:T(8,128)(2,1)}, bf16[2,1024,1024]{2,1,0:T(8,128)(2,1)}, s32[16,8,128]{2,1,0:T(8,128)}) custom-call(s32[16,8,128]{2,1,0:T(8,128)} %broadcast_in_dim.87.pos, bf16[1024,1024]{1,0:T(8,128)(2,1)} %x.3, f32[1,2048]{1,0:T(1,128)} %bitcast.54, bf16[2048,512]{1,0:T(8,128)(2,1)} %wq_hbm.1, bf16[2048,512]{1,0:T(8,128)(2,1)} %wkv_hbm.1, ...), custom_call_target="tpu_custom_call" | custom-call | tf_op jit(solution)/shard_map/qkv/pallas_call | solution.py:425
  28.2 2.9 %move_units.2 = bf16[1024,768]{1,0:T(8,128)(2,1)} custom-call(s32[32]{0:T(128)} %get-tuple-element.12.source_of, bf16[1024,768]{1,0:T(8,128)(2,1)} %get-tuple-element.9.came), custom_call_target="tpu_custom_call" | custom-call | tf_op jit(solution)/shard_map/move_units/pallas_call | solution.py:229
  31.0 6.0 %all-to-all-start = ((bf16[16,64,768]{2,1,0:T(8,128)(2,1)}), bf16[16,64,768]{2,1,0:T(8,128)(2,1)S(1)}, u32[]{:S(2)}, u32[]{:S(2)}) async-start(bf16[16,64,768]{2,1,0:T(8,128)(2,1)} %bitcast.46), calls=%async_computation | async-start | bytes 3145728 | tf_op jit(solution)/shard_map/all_to_all | solution.py:458
  37.1 0.2 all-gather.2.cloned.1.call-start
  37.3 0.5 all-gather.2.cloned.1.call-update
  37.8 0.5 slice.21
  39.0 0.1 add_select_fusion
  39.0 0.3 reduce-window.9
  39.3 0.1 slice.24
  39.4 0.1 pad.10.clone
  39.5 0.1 pad.7.clone
  39.6 0.9 slice_reduce_fusion
  40.4 0.1 eq.93
  40.6 0.1 slice_reduce_fusion.1
  40.7 0.1 fusion.4
  40.7 1.9 %multiply_sine_fusion = (f32[1024,32]{1,0:T(8,128)S(1)}, f32[1024,32]{1,0:T(8,128)S(1)}) fusion(f32[1024]{0:T(1024)S(1)} %get-tuple-element.14, f32[32]{0:T(128)S(1)} %multiply_power_fusion), kind=kLoop, calls=%fused_computation | loop fusion | flops 32768 | bytes 266368 | tf_op jit(solution)/shard_map/sin | solution.py:467
  42.6 0.2 copy.27
  42.8 0.1 tile.14
  42.9 1.0 copy.29.cosq
  43.9 0.2 copy.28
  44.0 0.1 tile.31
  44.1 1.0 copy.30.sinq
  45.1 1.0 copy.31.starts
  46.1 0.7 select_reduce_fusion.1.slot_of
  46.8 0.5 broadcast_maximum_fusion.1.pos_of
  47.4 0.6 select_convert_fusion.rot
  48.0 1.3 maximum_maximum_fusion
  49.3 25.7 %all-to-all-done = bf16[16,64,768]{2,1,0:T(8,128)(2,1)S(1)} async-done(((bf16[16,64,768]{2,1,0:T(8,128)(2,1)}), bf16[16,64,768]{2,1,0:T(8,128)(2,1)S(1)}, u32[]{:S(2)}, u32[]{:S(2)}) %all-to-all-start) | async-done | bytes 1572896 | tf_op jit(solution)/shard_map/all_to_all | solution.py:458
  75.0 1.1 copy-done
  76.2 11.3 %attention.1 = (bf16[8,128,256]{2,1,0:T(8,128)(2,1)}, bf16[1024,512]{1,0:T(8,128)(2,1)}) custom-call(s32[32]{0:T(128)} %select_reduce_fusion.1.slot_of, s32[32]{0:T(128)} %broadcast_maximum_fusion.1.pos_of, s32[8]{0:T(128)} %bitcast.56, bf16[1024,768]{1,0:T(8,128)(2,1)} %bitcast.45, f32[1024,128]{1,0:T(8,128)} %copy.29.cosq, f32[1024,128]{1,0:T(8,128)} %copy.30.sinq, ...), custom_call_target="tpu_custom_call" | custom-call | tf_op jit(solution)/shard_map/attention/pallas_call | solution.py:480
  87.5 6.2 %all-to-all-start.1 = ((bf16[16,64,512]{2,1,0:T(8,128)(2,1)}), bf16[16,64,512]{2,1,0:T(8,128)(2,1)S(1)}, u32[]{:S(2)}, u32[]{:S(2)}) async-start(bf16[16,64,512]{2,1,0:T(8,128)(2,1)} %bitcast.50), calls=%async_computation.1 | async-start | bytes 2097152 | tf_op jit(solution)/shard_map/all_to_all | solution.py:502
  93.7 0.6 multiply_add_fusion.source_of
  94.2 25.0 %all-to-all-done.1 = bf16[16,64,512]{2,1,0:T(8,128)(2,1)S(1)} async-done(((bf16[16,64,512]{2,1,0:T(8,128)(2,1)}), bf16[16,64,512]{2,1,0:T(8,128)(2,1)S(1)}, u32[]{:S(2)}, u32[]{:S(2)}) %all-to-all-start.1) | async-done | bytes 1048608 | tf_op jit(solution)/shard_map/all_to_all | solution.py:502
  119.2 1.0 copy-done.1
  120.2 2.5 %move_units.3.came = bf16[1024,512]{1,0:T(8,128)(2,1)} custom-call(s32[32]{0:T(128)} %multiply_add_fusion.source_of, bf16[1024,512]{1,0:T(8,128)(2,1)} %bitcast.47), custom_call_target="tpu_custom_call" | custom-call | tf_op jit(solution)/shard_map/move_units/pallas_call | solution.py:229
  122.6 51.4 %ffn.1 = bf16[1024,1024]{1,0:T(8,128)(2,1)} custom-call(bf16[2,1024,1024]{2,1,0:T(8,128)(2,1)} %get-tuple-element.7.xg, bf16[1024,512]{1,0:T(8,128)(2,1)} %move_units.3.came, bf16[1024,2048]{1,0:T(8,128)(2,1)} %all-gather.2.cloned.1.call-done.wo, f32[1,2048]{1,0:T(1,128)} %bitcast.55, bf16[2048,2560]{1,0:T(8,128)(2,1)} %wg.1, bf16[2048,2560]{1,0:T(8,128)(2,1)} %wu.1, ...), custom_call_target="tpu_custom_call" | custom-call | tf_op jit(solution)/shard_map/ffn/pallas_call | solution.py:513
  174.0 3.1 %copy.33 = bf16[1024,1024]{1,0:T(8,128)(2,1)} copy(bf16[1024,1024]{1,0:T(8,128)(2,1)} %ffn.1) | data formatting | bytes 4194304
  (17 shorter events, 0.1 us)
Async XLA Ops:
  31.0 6.8 %copy-start.2 = (s32[1,1024]{1,0:T(1,128)S(1)}, s32[1,1024]{1,0:T(1,128)}, u32[]{:S(2)}) copy-start(s32[1,1024]{1,0:T(1,128)} %param.16) | copy-start | bytes 12292
  31.0 44.0 %all-to-all-start = ((bf16[16,64,768]{2,1,0:T(8,128)(2,1)}), bf16[16,64,768]{2,1,0:T(8,128)(2,1)S(1)}, u32[]{:S(2)}, u32[]{:S(2)}) async-start(bf16[16,64,768]{2,1,0:T(8,128)(2,1)} %bitcast.46), calls=%async_computation | async-start | bytes 3145728 | tf_op jit(solution)/shard_map/all_to_all | solution.py:458
  37.1 85.6 %all-gather.2.cloned.1.call-start = ((), (), s32[]{:S(2)}) async-start(), calls=%async_computation.2 | async-start | bytes 6291456 | tf_op jit(solution)/shard_map/all_gather | solution.py:390
  75.0 1.1 copy-start
  87.5 6.2 %copy-start.3 = (s32[1,32]{1,0:T(1,128)S(1)}, s32[1,32]{1,0:T(1,128)}, u32[]{:S(2)}) copy-start(s32[1,32]{1,0:T(1,128)} %param.15) | copy-start | bytes 388
  87.5 31.7 %all-to-all-start.1 = ((bf16[16,64,512]{2,1,0:T(8,128)(2,1)}), bf16[16,64,512]{2,1,0:T(8,128)(2,1)S(1)}, u32[]{:S(2)}, u32[]{:S(2)}) async-start(bf16[16,64,512]{2,1,0:T(8,128)(2,1)} %bitcast.50), calls=%async_computation.1 | async-start | bytes 2097152 | tf_op jit(solution)/shard_map/all_to_all | solution.py:502
  119.2 1.0 copy-start.1
Sparse Core Ops, SparseCore 0:
  39.4 15.1 all-gather.1
